TPU v7x, 128 devices: a whole 4x4x4 slice. The times are simulated.
128 devices in a mesh: doc: 16 (over y, z), own: 8 (over x, core).
Axes of the slice: x: 4, y: 4, z: 4, core: 2. Of those that a mesh axis runs over, the one named last changes fastest.
Arguments:
- embeddings: bfloat16 [65536, 768], P(('doc', 'own')), may hold values from -6 to 6
- cluster_ids: int32 [65536], P(('doc', 'own')), may hold values from 0 to 50175, as said below
- keep_flags: int32 [65536], P(('doc', 'own')), may hold values 0 or 1
Outputs:
- centroids: bfloat16 [50176, 768], P(('doc', 'own'))
- scores: float32 [65536], P(('doc', 'own'))
Inputs may be any that keep to these rules, and one draw needn't show every extreme that they name: `cluster_ids`: cluster c is held by device c // 392 of the rows' order. Among the rows of one device, at most 8 name clusters held by any one device, and exactly 8 do for one device.
All inputs are finite; a program needn't handle non-finite values. No bound on the sum of `keep_flags` on one device may be relied on, other than what follows from the above.
Results may differ from a plain program's by a relative error of at most 0.0015.
Values may be sent and summed in bfloat16 or wider, within the bound.
No kernel may reach another device: no remote copies, remote signals or barrier semaphores. Data moves between devices by JAX's collectives and lax.ppermute only.
A program may use at most 64 MiB of HBM per device.

v0:
```python
import math

import jax
import jax.numpy as jnp
from jax import lax
from jax.sharding import PartitionSpec as P

CLUSTER_DEV = 392


def unit_rows(sums, width):
    inv_scale = lax.rsqrt(jnp.mean(sums * sums, axis=1, keepdims=True) + 1e-06) / math.sqrt(width)
    return (sums * inv_scale).astype(jnp.bfloat16)


def pack_rows(embeddings, slot_code, slot, slots_total):
    width = embeddings.shape[1]
    outgoing = jnp.zeros((slots_total, width), jnp.bfloat16).at[slot].set(embeddings)
    codes_out = jnp.full((slots_total,), -1, jnp.int32).at[slot].set(slot_code)
    return (outgoing, codes_out)


def body(embeddings, cluster_ids, keep_flags):
    row_count = embeddings.shape[0]
    width = embeddings.shape[1]
    grid_size = lax.axis_size(("doc", "own"))
    doc_count = lax.axis_size("doc")
    own_count = lax.axis_size("own")
    capacity = 2 * row_count // grid_size
    slots_total = grid_size * capacity
    per_device = CLUSTER_DEV
    target = cluster_ids // per_device
    local_id = cluster_ids % per_device
    hits = (target[:, None] == jnp.arange(grid_size, dtype=jnp.int32)[None, :]).astype(jnp.int32)
    position = jnp.sum(jnp.cumsum(hits, axis=0) * hits, axis=1) - 1
    slot_code = local_id + per_device * keep_flags
    row_scale = lax.rsqrt(
        jnp.mean(jnp.square(embeddings.astype(jnp.float32)), axis=1) + 1e-06
    ) / math.sqrt(width)
    slot = (target % own_count * doc_count + target // own_count) * capacity + position
    outgoing, codes_out = pack_rows(embeddings, slot_code, slot, slots_total)
    arrived, codes_in = (
        lax.all_to_all(outgoing, "own", split_axis=0, concat_axis=0, tiled=True),
        lax.all_to_all(codes_out, "own", split_axis=0, concat_axis=0, tiled=True),
    )
    slot_doc = jnp.arange(slots_total, dtype=jnp.int32) // capacity % doc_count
    valid = codes_in >= 0
    owner_index = jnp.where(valid, slot_doc * per_device + codes_in % per_device, -1)
    weight = jnp.where(valid, codes_in // per_device, 0)
    labels = jnp.arange(per_device * lax.axis_size("doc"), dtype=jnp.int32)
    table = ((labels[:, None] == owner_index[None, :]) * weight[None, :]).astype(jnp.bfloat16)
    sums = lax.psum_scatter(
        jnp.dot(table, arrived, preferred_element_type=jnp.float32),
        "doc",
        scatter_dimension=0,
        tiled=True,
    )
    centroids = unit_rows(sums, width)
    piece = lax.all_gather(centroids, "doc", axis=0, tiled=True)
    similar = jnp.dot(arrived, piece.T, preferred_element_type=jnp.float32)
    column = owner_index - jnp.int32(0)
    chosen = column[:, None] == jnp.arange(piece.shape[0], dtype=jnp.int32)[None, :]
    products = jnp.sum(jnp.where(chosen, similar, 0.0), axis=1)
    returned = lax.all_to_all(products, "own", split_axis=0, concat_axis=0, tiled=True)
    scores = returned[slot] * row_scale
    return (centroids, scores)


def solution(mesh):
    in_specs = (P(("doc", "own"), None), P(("doc", "own")), P(("doc", "own")))
    out_specs = (P(("doc", "own"), None), P(("doc", "own")))
    return jax.shard_map(body, mesh=mesh, in_specs=in_specs, out_specs=out_specs, check_vma=False)
```

profile of v0, /device:TPU:1, one launch (start us, length us, event | category | flops | bytes accessed | tf_op | source)
XLA Modules:
  0.0 299.3 jit_solution(1905121783948206056)
XLA Ops:
  7.2 0.0 copy-start.1
  7.2 0.8 fusion.25
  8.0 0.1 copy.7
  8.1 0.2 fusion.7
  8.4 0.2 fusion.6
  8.6 3.0 %scatter_custom_fusion = s32[1024]{0:T(1024)} fusion(s32[512]{0:T(512)S(1)} %compare_select_fusion, s32[512]{0:T(512)S(1)} %get-tuple-element.4, s32[]{:T(128)} %constant.95.clone.1), kind=kCustom, calls=%fused_computation.66 | custom fusion | bytes 4100 | tf_op jit(solution)/shard_map/scatter | solution.py:19
  11.7 5.8 %all-to-all-start = ((s32[8,128,1]{1,2,0:T(1,128)}), s32[8,128,1]{1,2,0:T(1,128)S(1)}, u32[]{:S(2)}, u32[]{:S(2)}) async-start(s32[8,128,1]{1,2,0:T(1,128)} %bitcast.5), calls=%async_computation | async-start | bytes 8192 | tf_op jit(solution)/shard_map/all_to_all | solution.py:44
  17.5 0.0 copy-done.1
  17.5 3.8 %scatter_custom_fusion.1 = bf16[1024,768]{1,0:T(8,128)(2,1)} fusion(s32[512]{0:T(512)S(1)} %compare_select_fusion, bf16[512,768]{1,0:T(8,128)(2,1)S(1)} %copy-done.1, bf16[]{:T(256)} %constant.105.clone.1), kind=kCustom, calls=%fused_computation.14 | custom fusion | bytes 1572866 | tf_op jit(solution)/shard_map/scatter | solution.py:18
  21.3 0.7 all-to-all-done
  22.0 4.2 %all-to-all-start.1 = ((bf16[8,128,768]{2,1,0:T(8,128)(2,1)}), bf16[8,128,768]{2,1,0:T(8,128)(2,1)S(1)}, u32[]{:S(2)}, u32[]{:S(2)}) async-start(bf16[8,128,768]{2,1,0:T(8,128)(2,1)} %bitcast.14), calls=%async_computation.1 | async-start | bytes 3145728 | tf_op jit(solution)/shard_map/all_to_all | solution.py:43
  26.1 0.0 reduce-scatter.4.cloned.1.call-start
  26.2 20.7 %all-to-all-done.1 = bf16[8,128,768]{2,1,0:T(8,128)(2,1)S(1)} async-done(((bf16[8,128,768]{2,1,0:T(8,128)(2,1)}), bf16[8,128,768]{2,1,0:T(8,128)(2,1)S(1)}, u32[]{:S(2)}, u32[]{:S(2)}) %all-to-all-start.1) | async-done | bytes 1572896 | tf_op jit(solution)/shard_map/all_to_all | solution.py:43
  46.9 13.4 %fusion = f32[6272,768]{1,0:T(8,128)} fusion(bf16[1024,768]{1,0:T(8,128)(2,1)S(1)} %bitcast.53, s32[1024]{0:T(1024)S(1)} %get-tuple-element.3, s32[1024]{0:T(1024)S(1)} %get-tuple-element.2), kind=kOutput, calls=%fused_computation.7 | convolution fusion | flops 9884270592 | bytes 20848640 | tf_op jit(solution)/shard_map/dot_general | solution.py:53
  60.2 0.0 reduce-scatter.4.cloned.1.call-update
  60.2 0.0 all-gather.2.cloned.1.call-start
  60.3 124.5 %reduce-scatter.4.cloned.1.call-done = f32[392,768]{1,0:T(8,128)} async-done(((f32[6272,768]{1,0:T(8,128)}), f32[392,768]{1,0:T(8,128)}) %reduce-scatter.4.cloned.1.call-update) | async-done | bytes 1204240
  184.8 0.0 copy-start
  184.8 1.5 multiply_reduce_fusion.1
  186.4 0.1 copy-done
  186.5 0.9 multiply_convert_fusion
  187.4 0.0 all-gather.2.cloned.1.call-update
  187.5 0.2 multiply_reduce_fusion
  187.7 76.4 %all-gather.2.cloned.1.call-done = bf16[6272,768]{1,0:T(8,128)(2,1)} async-done(((bf16[392,768]{1,0:T(8,128)(2,1)}), bf16[6272,768]{1,0:T(8,128)(2,1)}) %all-gather.2.cloned.1.call-update) | async-done | bytes 9633808 | tf_op jit(solution)/shard_map/all_gather | solution.py:59
  264.1 16.0 %select_reduce_fusion = f32[1024]{0:T(1024)} fusion(bf16[1024,768]{1,0:T(8,128)(2,1)S(1)} %bitcast.54, bf16[6272,768]{1,0:T(8,128)(2,1)} %all-gather.2.cloned.1.call-done, s32[1024]{0:T(1024)S(1)} %get-tuple-element.2), kind=kOutput, calls=%fused_computation.3 | convolution fusion | flops 9884269568 | bytes 11214848 | tf_op jit(solution)/shard_map/dot_general | solution.py:60
  280.1 4.9 %all-to-all-start.2 = ((f32[8,128,1]{1,2,0:T(1,128)}), f32[8,128,1]{1,2,0:T(1,128)S(1)}, u32[]{:S(2)}, u32[]{:S(2)}) async-start(f32[8,128,1]{1,2,0:T(1,128)} %bitcast.17), calls=%async_computation.2 | async-start | bytes 8192 | tf_op jit(solution)/shard_map/all_to_all | solution.py:64
  285.0 4.6 %all-to-all-done.2 = f32[8,128,1]{1,2,0:T(1,128)S(1)} async-done(((f32[8,128,1]{1,2,0:T(1,128)}), f32[8,128,1]{1,2,0:T(1,128)S(1)}, u32[]{:S(2)}, u32[]{:S(2)}) %all-to-all-start.2) | async-done | bytes 4128 | tf_op jit(solution)/shard_map/all_to_all | solution.py:64
  289.6 2.3 gather_fusion
  291.8 0.6 multiply_multiply_fusion
  (10 shorter events, 0.1 us)
Async XLA Ops:
  7.2 10.3 %copy-start.1 = (bf16[512,768]{1,0:T(8,128)(2,1)S(1)}, bf16[512,768]{1,0:T(8,128)(2,1)}, u32[]{:S(2)}) copy-start(bf16[512,768]{1,0:T(8,128)(2,1)} %param.3) | copy-start | bytes 2359300
  11.7 10.3 %all-to-all-start = ((s32[8,128,1]{1,2,0:T(1,128)}), s32[8,128,1]{1,2,0:T(1,128)S(1)}, u32[]{:S(2)}, u32[]{:S(2)}) async-start(s32[8,128,1]{1,2,0:T(1,128)} %bitcast.5), calls=%async_computation | async-start | bytes 8192 | tf_op jit(solution)/shard_map/all_to_all | solution.py:44
  22.0 24.9 %all-to-all-start.1 = ((bf16[8,128,768]{2,1,0:T(8,128)(2,1)}), bf16[8,128,768]{2,1,0:T(8,128)(2,1)S(1)}, u32[]{:S(2)}, u32[]{:S(2)}) async-start(bf16[8,128,768]{2,1,0:T(8,128)(2,1)} %bitcast.14), calls=%async_computation.1 | async-start | bytes 3145728 | tf_op jit(solution)/shard_map/all_to_all | solution.py:43
  26.1 158.7 %reduce-scatter.4.cloned.1.call-start = ((), (), s32[]{:S(2)}) async-start(), calls=%async_computation.5 | async-start | bytes 20471808
  60.2 203.9 %all-gather.2.cloned.1.call-start = ((), (), s32[]{:S(2)}) async-start(), calls=%async_computation.4 | async-start | bytes 10235904 | tf_op jit(solution)/shard_map/all_gather | solution.py:59
  184.8 1.6 copy-start
  280.1 9.5 %all-to-all-start.2 = ((f32[8,128,1]{1,2,0:T(1,128)}), f32[8,128,1]{1,2,0:T(1,128)S(1)}, u32[]{:S(2)}, u32[]{:S(2)}) async-start(f32[8,128,1]{1,2,0:T(1,128)} %bitcast.17), calls=%async_computation.2 | async-start | bytes 8192 | tf_op jit(solution)/shard_map/all_to_all | solution.py:64
Sparse Core Ops, SparseCore 0:
  60.4 124.4 reduce-scatter.3
  187.8 76.2 all-gather.1
where the time goes:
time: 300 us; the launch traced here: 299 us
  waiting for transfers between devices  227 us (76%)
  matrix products  29.3 us (10%)
  starting transfers between devices  14.9 us (5%)
  between operations  14.1 us (5%)
  local copies, waits for them, and re-layouts  9.33 us (3%)
  other arithmetic  4.63 us (2%)
    unnamed x3, waiting for transfers between devices  125 us
    all_gather x1, waiting for transfers between devices, body(): piece = lax.all_gather(centroids, 'doc', axis=0, tiled=True)  76.4 us
    all_to_all x1, waiting for transfers between devices, body(): lax.all_to_all(outgoing, 'own', split_axis=0, concat_axis=0, tiled=True)  20.7 us
    dot_general x1, matrix products, body(): similar = jnp.dot(arrived, piece.T, preferred_element_type=jnp.float32)  16 us
    dot_general x1, matrix products, body(): jnp.dot(table, arrived, preferred_element_type=jnp.float32)  13.4 us
  transfers between devices with their start and end apart: 5, of which 5 were waited for; matrix products, arithmetic and copies ran while one was open for 1% of the time, Pallas kernels for 0%

commit v1 on v0

v1 whole, which is shorter than its diff:
```python
import math

import jax
import jax.numpy as jnp
from jax import lax
from jax.sharding import PartitionSpec as P

CLUSTER_DEV = 392
AXES = ("doc", "own")
CODE_BASE = 16
CODE_LANES = 128


def body(embeddings, cluster_ids, keep_flags):
    row_count, width = embeddings.shape
    grid_size = lax.axis_size(AXES)
    capacity = 2 * row_count // grid_size
    slots_total = grid_size * capacity
    target = cluster_ids // CLUSTER_DEV
    local_id = cluster_ids % CLUSTER_DEV
    hits = (target[:, None] == jnp.arange(grid_size, dtype=jnp.int32)[None, :]).astype(jnp.bfloat16)
    rows = jnp.arange(row_count, dtype=jnp.int32)
    earlier = (rows[:, None] > rows[None, :]).astype(jnp.bfloat16)
    before = jnp.dot(earlier, hits, preferred_element_type=jnp.float32)
    position = jnp.sum(before * hits.astype(jnp.float32), axis=1).astype(jnp.int32)
    slot = target * capacity + position
    place = (jnp.arange(slots_total, dtype=jnp.int32)[:, None] == slot[None, :]).astype(jnp.bfloat16)
    lane = jnp.arange(CODE_LANES, dtype=jnp.int32)[None, :]
    codes = jnp.where(lane == 0, local_id[:, None] // CODE_BASE + 1, 0)
    codes = jnp.where(lane == 1, local_id[:, None] % CODE_BASE, codes)
    codes = jnp.where(lane == 2, keep_flags[:, None], codes)
    wide = jnp.concatenate([embeddings, codes.astype(jnp.bfloat16)], axis=1)
    outgoing = jnp.dot(place, wide, preferred_element_type=jnp.float32).astype(jnp.bfloat16)
    arrived = lax.all_to_all(outgoing, AXES, split_axis=0, concat_axis=0, tiled=True)
    row_scale = lax.rsqrt(
        jnp.mean(jnp.square(embeddings.astype(jnp.float32)), axis=1) + 1e-06
    ) / math.sqrt(width)
    code = arrived[:, width:width + 3].astype(jnp.int32)
    arrived = arrived[:, :width]
    owner = code[:, 0] * CODE_BASE + code[:, 1] - CODE_BASE
    labels = jnp.arange(CLUSTER_DEV, dtype=jnp.int32)
    match = labels[:, None] == owner[None, :]
    table = jnp.where(match, code[:, 2][None, :], 0).astype(jnp.bfloat16)
    sums = jnp.dot(table, arrived, preferred_element_type=jnp.float32)
    inv_scale = lax.rsqrt(jnp.mean(sums * sums, axis=1, keepdims=True) + 1e-06) / math.sqrt(width)
    centroids = (sums * inv_scale).astype(jnp.bfloat16)
    similar = lax.dot_general(
        centroids, arrived, (((1,), (1,)), ((), ())), preferred_element_type=jnp.float32
    )
    products = jnp.sum(jnp.where(match, similar, 0.0), axis=0)
    returned = lax.all_to_all(products, AXES, split_axis=0, concat_axis=0, tiled=True)
    scores = returned[slot] * row_scale
    return (centroids, scores)


def solution(mesh):
    in_specs = (P(AXES, None), P(AXES), P(AXES))
    out_specs = (P(AXES, None), P(AXES))
    return jax.shard_map(body, mesh=mesh, in_specs=in_specs, out_specs=out_specs, check_vma=False)
```

time: 300 us -> 67.5 us (0.23)
  waiting for transfers between devices: 227 us -> 37.2 us
  matrix products: 29.3 us -> 5.78 us
  between operations: 14.1 us -> 0.75 us
  local copies, waits for them, and re-layouts: 9.33 us -> 3.6 us
    unnamed x3 -> x0, waiting for transfers between devices: 125 us -> none
    all_gather x1 -> x0, waiting for transfers between devices: 76.4 us -> none  [body(): piece = lax.all_gather(centroids, 'doc', axis=0, tiled=True)]
    dot_general x2 -> x4, matrix products: 29.3 us -> 5.78 us  [the longest x1 3.64 us: body(): jnp.dot(place, wide, preferred_element_type=jnp.float32)]
    all_to_all x3 -> x2, waiting for transfers between devices: 26 us -> 37.2 us  [the longest x1 27.5 us: body(): lax.all_to_all(outgoing, AXES, split_axis=0, concat_axis=0, tiled=True)]
    scatter x2 -> x0, local copies, waits for them, and re-layouts: 6.82 us -> none  [the longest x1 3.8 us: pack_rows(): jnp.zeros((slots_total, width), jnp.bfloat16).at[slot].set(embeddings)]
    all_to_all x3 -> x2, starting transfers between devices: 14.9 us -> 15.8 us  [the longest x1 11.5 us: body(): lax.all_to_all(outgoing, AXES, split_axis=0, concat_axis=0, tiled=True)]
  transfers between devices with their start and end apart: 5 -> 2, of which waited for: 5 -> 2; matrix products, arithmetic and copies ran while one was open for 1% -> 0% of each run, Pallas kernels for 0% -> 0%
where the time goes in v1:
time: 67.5 us; the launch traced here: 67.2 us
  waiting for transfers between devices  37.2 us (55%)
  starting transfers between devices  15.8 us (23%)
  matrix products  5.78 us (9%)
  other arithmetic  4.14 us (6%)
  local copies, waits for them, and re-layouts  3.6 us (5%)
  between operations  0.75 us (1%)
    all_to_all x1, waiting for transfers between devices, body(): lax.all_to_all(outgoing, AXES, split_axis=0, concat_axis=0, tiled=True)  27.5 us
    all_to_all x1, starting transfers between devices, body(): lax.all_to_all(outgoing, AXES, split_axis=0, concat_axis=0, tiled=True)  11.5 us
    all_to_all x1, waiting for transfers between devices, body(): lax.all_to_all(products, AXES, split_axis=0, concat_axis=0, tiled=True)  9.62 us
    all_to_all x1, starting transfers between devices, body(): lax.all_to_all(products, AXES, split_axis=0, concat_axis=0, tiled=True)  4.28 us
    dot_general x1, matrix products, body(): jnp.dot(place, wide, preferred_element_type=jnp.float32)  3.64 us
    gather x1, local copies, waits for them, and re-layouts, body(): scores = returned[slot] * row_scale  2.29 us
  transfers between devices with their start and end apart: 2, of which 2 were waited for; matrix products, arithmetic and copies ran while one was open for 0% of the time, Pallas kernels for 0%

profile of v1, /device:TPU:1, one launch (start us, length us, event | category | flops | bytes accessed | tf_op | source)
XLA Modules:
  0.0 67.2 jit_solution(18175161758417937373)
XLA Ops:
  0.7 0.7 %add_select_fusion.1 = (s32[512]{0:T(512)S(1)}, s32[512]{0:T(512)S(1)}, s32[512]{0:T(512)S(1)}) fusion(s32[512]{0:T(512)} %param.4), kind=kLoop, calls=%fused_computation.37 | loop fusion | flops 16384 | bytes 8192 | tf_op jit(solution)/shard_map/jit(remainder)/select_n | solution.py:30
  1.4 0.3 fusion.4
  1.7 1.0 %select_convert_fusion.2 = bf16[512,128]{1,0:T(8,128)(2,1)S(1)} fusion(s32[512]{0:T(512)S(1)} %get-tuple-element.7, s32[512]{0:T(512)S(1)} %get-tuple-element.6, s32[512]{0:T(512)} %param.5, pred[128]{0:T(512)(128)(4,1)S(1)} %get-tuple-element.11, pred[128]{0:T(512)(128)(4,1)S(1)} %get-tuple-element.12, pred[128]{0:T(512)(128)(4,1)S(1)} %iota_compare_fusion.11), kind=kLoop, calls=%fused_computation.29 | loop fusion | flops 262144 | bytes 137600 | tf_op jit(solution)/shard_map/convert_element_type | solution.py:32
  2.6 3.6 %convert_bitcast_fusion = bf16[128,8,896]{2,1,0:T(8,128)(2,1)} fusion(s32[512]{0:T(512)S(1)} %get-tuple-element.5, bf16[512,128]{1,0:T(8,128)(2,1)S(1)} %select_convert_fusion.2, bf16[512,768]{1,0:T(8,128)(2,1)} %param.3), kind=kOutput, calls=%fused_computation.3 | convolution fusion | flops 942800896 | bytes 2754560 | tf_op jit(solution)/shard_map/dot_general | solution.py:33
  6.3 0.0 copy-start
  6.3 11.5 %all-to-all-start = ((bf16[128,8,896]{2,1,0:T(8,128)(2,1)}), bf16[128,8,896]{2,1,0:T(8,128)(2,1)S(1)}, u32[]{:S(2)}, u32[]{:S(2)}) async-start(bf16[128,8,896]{2,1,0:T(8,128)(2,1)} %convert_bitcast_fusion), calls=%async_computation | async-start | bytes 3670016 | tf_op jit(solution)/shard_map/all_to_all | solution.py:34
  17.8 0.0 copy-done
  17.8 0.2 multiply_reduce_fusion
  18.0 27.5 %all-to-all-done = bf16[128,8,896]{2,1,0:T(8,128)(2,1)S(1)} async-done(((bf16[128,8,896]{2,1,0:T(8,128)(2,1)}), bf16[128,8,896]{2,1,0:T(8,128)(2,1)S(1)}, u32[]{:S(2)}, u32[]{:S(2)}) %all-to-all-start) | async-done | bytes 1835040 | tf_op jit(solution)/shard_map/all_to_all | solution.py:34
  45.6 0.1 slice_convert_fusion
  45.6 0.6 fusion.13
  46.3 1.0 %multiply_reduce_fusion.1 = (f32[392]{0:T(512)S(1)}, f32[392,768]{1,0:T(8,128)S(1)}) fusion(bf16[1024,896]{1,0:T(8,128)(2,1)S(1)} %bitcast.7, s32[1024]{0:T(1024)S(1)} %get-tuple-element.3, s32[1024]{0:T(1024)S(1)} %get-tuple-element.2), kind=kOutput, calls=%fused_computation.12 | convolution fusion | flops 618368640 | bytes 2786848 | tf_op jit(solution)/shard_map/dot_general | solution.py:44
  47.3 0.1 multiply_convert_fusion
  47.4 0.0 copy-start.1
  47.4 0.8 %select_reduce_fusion = f32[1024]{0:T(1024)S(1)} fusion(bf16[392,768]{1,0:T(8,128)(2,1)S(1)} %multiply_convert_fusion, bf16[1024,896]{1,0:T(8,128)(2,1)S(1)} %bitcast.8, s32[1024]{0:T(1024)S(1)} %get-tuple-element.2), kind=kOutput, calls=%fused_computation.4 | convolution fusion | flops 617765888 | bytes 2183168 | tf_op jit(solution)/shard_map/dot_general | solution.py:47
  48.3 0.0 copy-done.1
  48.3 0.7 %all_to_all.19 = f32[128,8,1]{1,0,2:T(8,128)} reshape(f32[1024]{0:T(1024)S(1)} %select_reduce_fusion) | data formatting | bytes 8192 | tf_op jit(solution)/shard_map/all_to_all | solution.py:51
  49.0 4.3 %all-to-all-start.1 = ((f32[128,8,1]{1,2,0:T(1,128)}), f32[128,8,1]{1,2,0:T(1,128)S(1)}, u32[]{:S(2)}, u32[]{:S(2)}) async-start(f32[128,8,1]{1,2,0:T(1,128)} %bitcast.2), calls=%async_computation.1 | async-start | bytes 131072 | tf_op jit(solution)/shard_map/all_to_all | solution.py:51
  53.3 9.6 %all-to-all-done.1 = f32[128,8,1]{1,2,0:T(1,128)S(1)} async-done(((f32[128,8,1]{1,2,0:T(1,128)}), f32[128,8,1]{1,2,0:T(1,128)S(1)}, u32[]{:S(2)}, u32[]{:S(2)}) %all-to-all-start.1) | async-done | bytes 4128 | tf_op jit(solution)/shard_map/all_to_all | solution.py:51
  62.9 0.5 broadcast.99
  63.4 0.8 %reduce.7 = f32[128,8]{1,0:T(8,128)S(1)} reduce(f32[128,8,1]{1,2,0:T(1,128)S(1)} %all-to-all-done.1, f32[]{:T(128)} %broadcast.99), dimensions={2}, to_apply=%all_to_all.20.reduce_sub_computation.3 | reduce | bytes 8196 | tf_op jit(solution)/shard_map/all_to_all | solution.py:51
  64.2 0.1 all_to_all.21
  64.3 2.3 %gather_fusion = f32[512]{0:T(512)S(1)} fusion(f32[1024]{0:T(1024)S(1)} %all_to_all.21, s32[1024]{0:T(1024)S(1)} %pad_clamp_fusion), kind=kCustom, calls=%fused_computation | custom fusion | bytes 6144 | tf_op jit(solution)/shard_map/gather | solution.py:52
  66.6 0.6 multiply_multiply_fusion
  (5 shorter events, 0.0 us)
Async XLA Ops:
  6.3 11.5 %copy-start = (bf16[512,768]{1,0:T(8,128)(2,1)S(1)}, bf16[512,768]{1,0:T(8,128)(2,1)}, u32[]{:S(2)}) copy-start(bf16[512,768]{1,0:T(8,128)(2,1)} %param.3) | copy-start | bytes 2359300
  6.3 39.3 %all-to-all-start = ((bf16[128,8,896]{2,1,0:T(8,128)(2,1)}), bf16[128,8,896]{2,1,0:T(8,128)(2,1)S(1)}, u32[]{:S(2)}, u32[]{:S(2)}) async-start(bf16[128,8,896]{2,1,0:T(8,128)(2,1)} %convert_bitcast_fusion), calls=%async_computation | async-start | bytes 3670016 | tf_op jit(solution)/shard_map/all_to_all | solution.py:34
  47.4 0.8 %copy-start.1 = (bf16[392,768]{1,0:T(8,128)(2,1)}, bf16[392,768]{1,0:T(8,128)(2,1)S(1)}, u32[]{:S(2)}) copy-start(bf16[392,768]{1,0:T(8,128)(2,1)S(1)} %multiply_convert_fusion) | copy-start | bytes 1806340
  49.0 13.9 %all-to-all-start.1 = ((f32[128,8,1]{1,2,0:T(1,128)}), f32[128,8,1]{1,2,0:T(1,128)S(1)}, u32[]{:S(2)}, u32[]{:S(2)}) async-start(f32[128,8,1]{1,2,0:T(1,128)} %bitcast.2), calls=%async_computation.1 | async-start | bytes 131072 | tf_op jit(solution)/shard_map/all_to_all | solution.py:51

commit v2 on v1

v2 whole, which is shorter than its diff:
```python
import math

import jax
import jax.numpy as jnp
from jax import lax
from jax.experimental import pallas as pl
from jax.experimental.pallas import tpu as pltpu
from jax.sharding import PartitionSpec as P

AXES = ("doc", "own")
CLUSTER_DEV = 392
CLUSTER_PAD = 400
DEVICES = 128
CAP = 8
SLOTS = DEVICES * CAP
ROWS = 512
WIDTH = 768
LANES = 128
WIDE = WIDTH + LANES
CODE_BASE = 16
PARTS = 4
PART = SLOTS // PARTS
PACK_VMEM = 63 * 1024 * 1024
VMEM_LIMIT = 48 * 1024 * 1024

NN = (((1,), (0,)), ((), ()))
NT = (((1,), (1,)), ((), ()))


def iota(shape, axis):
    return lax.broadcasted_iota(jnp.int32, shape, axis)


def matmul(a, b, dims=NN):
    return lax.dot_general(a, b, dims, preferred_element_type=jnp.float32)


def as_bf16(mask):
    return jnp.where(mask, 1.0, 0.0).astype(jnp.bfloat16)


def split3(x):
    high = x.astype(jnp.bfloat16)
    rest = x - high.astype(jnp.float32)
    middle = rest.astype(jnp.bfloat16)
    low = (rest - middle.astype(jnp.float32)).astype(jnp.bfloat16)
    return high, middle, low


def owner_device(ids):
    return ((ids >> 3) * 5350) >> 18


def pack_kernel(ids_ref, keep_ref, emb_hbm, out_hbm, slot_ref, emb, staged, in_sem, out_sem):
    load = pltpu.make_async_copy(emb_hbm, emb, in_sem)
    load.start()
    ids = ids_ref[...]
    target = owner_device(ids)
    local = ids - target * CLUSTER_DEV
    hits = iota((DEVICES, ROWS), 0) == target
    ones_bf = as_bf16(hits)
    earlier = as_bf16(iota((LANES, LANES), 0) < iota((LANES, LANES), 1))
    every = jnp.ones((LANES, LANES), jnp.bfloat16)
    before, offset = [], None
    for k in range(ROWS // LANES):
        block = ones_bf[:, k * LANES:(k + 1) * LANES]
        count = matmul(block, earlier)
        before.append(count if offset is None else count + offset)
        total = matmul(block, every)
        offset = total if offset is None else offset + total
    counts = jnp.concatenate(before, axis=1)
    position = jnp.sum(jnp.where(hits, counts, 0.0), axis=0, keepdims=True)
    slot = target * CAP + position.astype(jnp.int32)
    slot_ref[...] = slot
    row = iota((LANES, ROWS), 0)
    codes = jnp.where(row == 0, (local >> 4) + 1, 0)
    codes = jnp.where(row == 1, local & (CODE_BASE - 1), codes)
    codes = jnp.where(row == 2, keep_ref[...], codes)
    codes = codes.astype(jnp.float32).astype(jnp.bfloat16)
    load.wait()
    copies = []
    for k in range(PARTS):
        here = pl.ds(k * PART, PART)
        place = as_bf16(iota((PART, ROWS), 0) + k * PART == slot)
        staged[here, :WIDTH] = matmul(place, emb[...]).astype(jnp.bfloat16)
        staged[here, WIDTH:] = matmul(place, codes, NT).astype(jnp.bfloat16)
        copy = pltpu.make_async_copy(staged.at[here], out_hbm.at[here], out_sem.at[k])
        copy.start()
        copies.append(copy)
    for copy in copies:
        copy.wait()


def pack(embeddings, ids, keep):
    vmem = pl.BlockSpec(memory_space=pltpu.VMEM)
    hbm = pl.BlockSpec(memory_space=pltpu.HBM)
    return pl.pallas_call(
        pack_kernel,
        out_shape=(
            jax.ShapeDtypeStruct((SLOTS, WIDE), jnp.bfloat16),
            jax.ShapeDtypeStruct((1, ROWS), jnp.int32),
        ),
        in_specs=[vmem, vmem, hbm],
        out_specs=(hbm, vmem),
        scratch_shapes=[
            pltpu.VMEM((ROWS, WIDTH), jnp.bfloat16),
            pltpu.VMEM((SLOTS, WIDE), jnp.bfloat16),
            pltpu.SemaphoreType.DMA,
            pltpu.SemaphoreType.DMA((PARTS,)),
        ],
        compiler_params=pltpu.CompilerParams(vmem_limit_bytes=PACK_VMEM),
    )(ids, keep, embeddings)


def middle_kernel(arrived, centroids_hbm, products_ref, centroids, out_sem):
    pick = as_bf16(
        (iota((CAP, LANES), 0) == iota((CAP, LANES), 1))
    )
    codes = matmul(pick, arrived[:, WIDTH:], NT)
    owner = codes[0:1].astype(jnp.int32) * CODE_BASE + codes[1:2].astype(jnp.int32) - CODE_BASE
    keep = codes[2:3] > 0.5
    match = iota((CLUSTER_PAD, SLOTS), 0) == owner
    rows = arrived[:, :WIDTH]
    sums = matmul(as_bf16(match & keep), rows)
    inv_scale = lax.rsqrt(
        jnp.sum(sums * sums, axis=1, keepdims=True) * (1.0 / WIDTH) + 1e-06
    ) / math.sqrt(WIDTH)
    unit = (sums * inv_scale).astype(jnp.bfloat16)
    centroids[...] = unit[:CLUSTER_DEV]
    store = pltpu.make_async_copy(centroids, centroids_hbm, out_sem)
    store.start()
    similar = matmul(unit, rows, NT)
    products = jnp.sum(jnp.where(match, similar, 0.0), axis=0, keepdims=True)
    mine = iota((DEVICES, SLOTS), 1) // CAP == iota((DEVICES, SLOTS), 0)
    spread = as_bf16(iota((SLOTS, LANES), 0) % CAP == iota((SLOTS, LANES), 1))
    total = None
    for part in split3(products):
        term = matmul(jnp.where(mine, part.astype(jnp.float32), 0.0).astype(jnp.bfloat16), spread)
        total = term if total is None else total + term
    products_ref[...] = total
    store.wait()


def middle(arrived):
    vmem = pl.BlockSpec(memory_space=pltpu.VMEM)
    hbm = pl.BlockSpec(memory_space=pltpu.HBM)
    return pl.pallas_call(
        middle_kernel,
        out_shape=(
            jax.ShapeDtypeStruct((CLUSTER_DEV, WIDTH), jnp.bfloat16),
            jax.ShapeDtypeStruct((DEVICES, LANES), jnp.float32),
        ),
        in_specs=[vmem],
        out_specs=(hbm, vmem),
        scratch_shapes=[
            pltpu.VMEM((CLUSTER_DEV, WIDTH), jnp.bfloat16),
            pltpu.SemaphoreType.DMA,
        ],
        compiler_params=pltpu.CompilerParams(vmem_limit_bytes=VMEM_LIMIT),
    )(arrived)


def final_kernel(returned_ref, slot_ref, scale_ref, scores_ref):
    slot = slot_ref[...]
    hits = as_bf16(iota((DEVICES, ROWS), 0) == slot // CAP)
    back = returned_ref[...].T[:CAP]
    total = None
    for part in split3(back):
        term = matmul(part, hits)
        total = term if total is None else total + term
    chosen = jnp.where(iota((CAP, ROWS), 0) == slot % CAP, total, 0.0)
    scores_ref[...] = jnp.sum(chosen, axis=0, keepdims=True) * scale_ref[...]


def final(returned, slot, scale):
    vmem = pl.BlockSpec(memory_space=pltpu.VMEM)
    return pl.pallas_call(
        final_kernel,
        out_shape=jax.ShapeDtypeStruct((1, ROWS), jnp.float32),
        in_specs=[vmem] * 3,
        out_specs=vmem,
        compiler_params=pltpu.CompilerParams(vmem_limit_bytes=16 * 1024 * 1024),
    )(returned, slot, scale)


def body(embeddings, cluster_ids, keep_flags):
    outgoing, slot = pack(embeddings, cluster_ids.reshape(1, ROWS), keep_flags.reshape(1, ROWS))
    arrived = lax.all_to_all(outgoing, AXES, split_axis=0, concat_axis=0, tiled=True)
    row_scale = lax.rsqrt(
        jnp.mean(jnp.square(embeddings.astype(jnp.float32)), axis=1) + 1e-06
    ) / math.sqrt(WIDTH)
    centroids, products = middle(arrived)
    returned = lax.all_to_all(products, AXES, split_axis=0, concat_axis=0, tiled=True)
    scores = final(returned, slot, row_scale.reshape(1, ROWS))
    return (centroids, scores.reshape(ROWS))


def solution(mesh):
    in_specs = (P(AXES, None), P(AXES), P(AXES))
    out_specs = (P(AXES, None), P(AXES))
    return jax.shard_map(body, mesh=mesh, in_specs=in_specs, out_specs=out_specs, check_vma=False)
```

time: 67.5 us -> 62.8 us (0.930)
  Pallas kernels: 0 us -> 8.76 us
  matrix products: 5.78 us -> 0 us
  other arithmetic: 4.14 us -> 0.24 us
  local copies, waits for them, and re-layouts: 3.6 us -> 0.01 us
    pallas_call x0 -> x3, Pallas kernels: none -> 8.76 us  [the longest x1 4.49 us: pack(): pl.pallas_call(pack_kernel, out_shape=(jax.ShapeDtypeStruct((SLOTS, WIDE)...]
    dot_general x4 -> x0, matrix products: 5.78 us -> none  [the longest x1 3.64 us: body(): jnp.dot(place, wide, preferred_element_type=jnp.float32)]
    gather x1 -> x0, local copies, waits for them, and re-layouts: 2.29 us -> none  [body(): scores = returned[slot] * row_scale]
    all_to_all x3 -> x0, local copies, waits for them, and re-layouts: 1.31 us -> none  [body(): lax.all_to_all(products, AXES, split_axis=0, concat_axis=0, tiled=True)]
    convert_element_type x3 -> x0, other arithmetic: 1.15 us -> none  [the longest x1 0.95 us: body(): wide = jnp.concatenate([embeddings, codes.astype(jnp.bfloat16)], axis=1)]
    all_to_all x1 -> x0, other arithmetic: 0.81 us -> none  [body(): lax.all_to_all(products, AXES, split_axis=0, concat_axis=0, tiled=True)]
    select_n x2 -> x0, other arithmetic: 0.71 us -> none  [the longest x1 0.71 us: body(): codes = jnp.where(lane == 1, local_id[:, None] % CODE_BASE, codes)]
where the time goes in v2:
time: 62.8 us; the launch traced here: 62.6 us
  waiting for transfers between devices  37.1 us (59%)
  starting transfers between devices  15.8 us (25%)
  Pallas kernels  8.76 us (14%)
  between operations  0.69 us (1%)
    all_to_all x1, waiting for transfers between devices, body(): lax.all_to_all(outgoing, AXES, split_axis=0, concat_axis=0, tiled=True)  27.5 us
    all_to_all x1, starting transfers between devices, body(): lax.all_to_all(outgoing, AXES, split_axis=0, concat_axis=0, tiled=True)  11.5 us
    all_to_all x1, waiting for transfers between devices, body(): lax.all_to_all(products, AXES, split_axis=0, concat_axis=0, tiled=True)  9.57 us
    pallas_call x1, Pallas kernels, pack(): pl.pallas_call(pack_kernel, out_shape=(jax.ShapeDtypeStruct((SLOTS, WIDE)...  4.49 us
    all_to_all x1, starting transfers between devices, body(): lax.all_to_all(products, AXES, split_axis=0, concat_axis=0, tiled=True)  4.26 us
    pallas_call x1, Pallas kernels, middle(): pl.pallas_call(middle_kernel, out_shape=(jax.ShapeDtypeStruct((CLUSTER_DE...  3.46 us
  transfers between devices with their start and end apart: 2, of which 2 were waited for; matrix products, arithmetic and copies ran while one was open for 0% of the time, Pallas kernels for 0%

profile of v2, /device:TPU:1, one launch (start us, length us, event | category | flops | bytes accessed | tf_op | source)
XLA Modules:
  0.0 62.6 jit_solution(4365933528002464)
XLA Ops:
  0.6 4.5 %shard_map.50 = (bf16[1024,896]{1,0:T(8,128)(2,1)}, s32[1,512]{1,0:T(1,128)}) custom-call(s32[1,512]{1,0:T(1,128)} %bitcast.14, s32[1,512]{1,0:T(1,128)} %bitcast.15, bf16[512,768]{1,0:T(8,128)(2,1)} %emb_hbm.1), custom_call_target="tpu_custom_call" | custom-call | tf_op jit(solution)/shard_map/pallas_call | solution.py:97
  5.1 0.0 copy-start.1
  5.1 11.5 %all-to-all-start = ((bf16[128,8,896]{2,1,0:T(8,128)(2,1)}), bf16[128,8,896]{2,1,0:T(8,128)(2,1)S(1)}, u32[]{:S(2)}, u32[]{:S(2)}) async-start(bf16[128,8,896]{2,1,0:T(8,128)(2,1)} %bitcast.13), calls=%async_computation | async-start | bytes 3670016 | tf_op jit(solution)/shard_map/all_to_all | solution.py:188
  16.6 0.0 copy-done.1
  16.7 0.0 copy-start
  16.7 0.2 multiply_reduce_fusion
  16.9 27.5 %all-to-all-done = bf16[128,8,896]{2,1,0:T(8,128)(2,1)S(1)} async-done(((bf16[128,8,896]{2,1,0:T(8,128)(2,1)}), bf16[128,8,896]{2,1,0:T(8,128)(2,1)S(1)}, u32[]{:S(2)}, u32[]{:S(2)}) %all-to-all-start) | async-done | bytes 1835040 | tf_op jit(solution)/shard_map/all_to_all | solution.py:188
  44.4 3.5 %shard_map.51 = (bf16[392,768]{1,0:T(8,128)(2,1)}, f32[128,128]{1,0:T(8,128)}) custom-call(bf16[1024,896]{1,0:T(8,128)(2,1)S(1)} %bitcast.10), custom_call_target="tpu_custom_call" | custom-call | tf_op jit(solution)/shard_map/pallas_call | solution.py:147
  47.9 4.3 %all-to-all-start.1 = ((f32[128,1,128]{2,1,0:T(1,128)}), f32[128,1,128]{2,1,0:T(1,128)S(1)}, u32[]{:S(2)}, u32[]{:S(2)}) async-start(f32[128,1,128]{2,1,0:T(1,128)} %bitcast.5), calls=%async_computation.1 | async-start | bytes 131072 | tf_op jit(solution)/shard_map/all_to_all | solution.py:193
  52.2 9.6 %all-to-all-done.1 = f32[128,1,128]{2,1,0:T(1,128)S(1)} async-done(((f32[128,1,128]{2,1,0:T(1,128)}), f32[128,1,128]{2,1,0:T(1,128)S(1)}, u32[]{:S(2)}, u32[]{:S(2)}) %all-to-all-start.1) | async-done | bytes 65568 | tf_op jit(solution)/shard_map/all_to_all | solution.py:193
  61.7 0.0 copy-done
  61.7 0.8 %shard_map.52 = f32[1,512]{1,0:T(1,128)} custom-call(f32[128,128]{1,0:T(8,128)S(1)} %bitcast.11, s32[1,512]{1,0:T(1,128)S(1)} %copy-done, f32[1,512]{1,0:T(1,128)S(1)} %bitcast.12), custom_call_target="tpu_custom_call" | custom-call | tf_op jit(solution)/shard_map/pallas_call | solution.py:177
  (1 shorter events, 0.0 us)
Async XLA Ops:
  5.1 11.5 %copy-start.1 = (bf16[512,768]{1,0:T(8,128)(2,1)S(1)}, bf16[512,768]{1,0:T(8,128)(2,1)}, u32[]{:S(2)}) copy-start(bf16[512,768]{1,0:T(8,128)(2,1)} %emb_hbm.1) | copy-start | bytes 2359300
  5.1 39.3 %all-to-all-start = ((bf16[128,8,896]{2,1,0:T(8,128)(2,1)}), bf16[128,8,896]{2,1,0:T(8,128)(2,1)S(1)}, u32[]{:S(2)}, u32[]{:S(2)}) async-start(bf16[128,8,896]{2,1,0:T(8,128)(2,1)} %bitcast.13), calls=%async_computation | async-start | bytes 3670016 | tf_op jit(solution)/shard_map/all_to_all | solution.py:188
  16.7 45.1 %copy-start = (s32[1,512]{1,0:T(1,128)S(1)}, s32[1,512]{1,0:T(1,128)}, u32[]{:S(2)}) copy-start(s32[1,512]{1,0:T(1,128)} %get-tuple-element.9.slot_ref) | copy-start | bytes 6148
  47.9 13.8 %all-to-all-start.1 = ((f32[128,1,128]{2,1,0:T(1,128)}), f32[128,1,128]{2,1,0:T(1,128)S(1)}, u32[]{:S(2)}, u32[]{:S(2)}) async-start(f32[128,1,128]{2,1,0:T(1,128)} %bitcast.5), calls=%async_computation.1 | async-start | bytes 131072 | tf_op jit(solution)/shard_map/all_to_all | solution.py:193

commit v3 on v2

v3 whole, which is shorter than its diff:
```python
import math

import jax
import jax.numpy as jnp
from jax import lax
from jax.experimental import pallas as pl
from jax.experimental.pallas import tpu as pltpu
from jax.sharding import PartitionSpec as P

AXES = ("doc", "own")
CLUSTER_DEV = 392
CLUSTER_PAD = 400
DEVICES = 128
CAP = 8
SLOTS = DEVICES * CAP
ROWS = 512
WIDTH = 768
LANES = 128
SUB = 4
PER = CAP // SUB
DATA_TILES = WIDTH // LANES * PER
GROUP = LANES // CAP
CODE_BASE = 16
CODE_KEEP = 32
PARTS = 4
PART = SLOTS // PARTS
PART_PEERS = DEVICES // PARTS
PACK_VMEM = 63 * 1024 * 1024
VMEM_LIMIT = 48 * 1024 * 1024

NN = (((1,), (0,)), ((), ()))
NT = (((1,), (1,)), ((), ()))


def iota(shape, axis):
    return lax.broadcasted_iota(jnp.int32, shape, axis)


def matmul(a, b, dims=NN):
    return lax.dot_general(a, b, dims, preferred_element_type=jnp.float32)


def as_bf16(mask):
    return jnp.where(mask, 1.0, 0.0).astype(jnp.bfloat16)


def split3(x):
    high = x.astype(jnp.bfloat16)
    rest = x - high.astype(jnp.float32)
    middle = rest.astype(jnp.bfloat16)
    low = (rest - middle.astype(jnp.float32)).astype(jnp.bfloat16)
    return high, middle, low


def owner_device(ids):
    return ((ids >> 3) * 5350) >> 18


def pack_kernel(
    ids_hbm, keep_hbm, emb_hbm, out_hbm, slot_hbm, ids_ref, keep_ref, emb, staged, codes, slots, in_sem, out_sem
):
    loads = [
        pltpu.make_async_copy(source, kept, in_sem.at[k])
        for k, (source, kept) in enumerate(((ids_hbm, ids_ref), (keep_hbm, keep_ref), (emb_hbm, emb)))
    ]
    for load in loads:
        load.start()
    loads[0].wait()
    loads[1].wait()
    ids = ids_ref[...]
    target = owner_device(ids)
    local = ids - target * CLUSTER_DEV
    hits = iota((DEVICES, ROWS), 0) == target
    hits_bf = as_bf16(hits)
    earlier = as_bf16(iota((LANES, LANES), 0) < iota((LANES, LANES), 1))
    every = jnp.ones((LANES, LANES), jnp.bfloat16)
    before, offset = [], None
    blocks = ROWS // LANES
    for k in range(blocks):
        block = hits_bf[:, k * LANES:(k + 1) * LANES]
        count = matmul(block, earlier)
        before.append(count if offset is None else count + offset)
        if k < blocks - 1:
            total = matmul(block, every)
            offset = total if offset is None else offset + total
    counts = jnp.concatenate(before, axis=1)
    position = jnp.sum(jnp.where(hits, counts, 0.0), axis=0, keepdims=True).astype(jnp.int32)
    slot = target * CAP + position
    slots[...] = slot
    stores = [pltpu.make_async_copy(slots, slot_hbm, out_sem.at[0])]
    stores[-1].start()
    at_slot = iota((LANES, ROWS), 0) & (CAP - 1) == position
    upper = (local >> 4) + 1 + CODE_KEEP * keep_ref[...]
    lower = local & (CODE_BASE - 1)
    coded = [
        matmul(hits_bf, jnp.where(at_slot, part, 0).astype(jnp.float32).astype(jnp.bfloat16), NT)
        for part in (upper, lower)
    ]
    which = iota((DEVICES, SUB, LANES), 1)
    tile = jnp.where(which == 1, coded[1][:, None, :], 0.0)
    tile = jnp.where(which == 0, coded[0][:, None, :], tile)
    codes[...] = tile.astype(jnp.bfloat16)
    stores.append(pltpu.make_async_copy(codes, out_hbm.at[:, DATA_TILES], out_sem.at[1]))
    stores[-1].start()
    loads[2].wait()
    for k in range(PARTS):
        place = as_bf16(iota((PART, ROWS), 0) + k * PART == slot)
        block = matmul(place, emb[...]).astype(jnp.bfloat16)
        peers = pl.ds(k * PART_PEERS, PART_PEERS)
        for c in range(WIDTH // LANES):
            piece = block[:, c * LANES:(c + 1) * LANES].reshape(PART_PEERS, PER, SUB, LANES)
            staged[peers, c * PER:(c + 1) * PER] = piece
        stores.append(
            pltpu.make_async_copy(staged.at[peers], out_hbm.at[peers, pl.ds(0, DATA_TILES)], out_sem.at[2 + k])
        )
        stores[-1].start()
    for store in stores:
        store.wait()


def pack(ids, keep, embeddings):
    hbm = pl.BlockSpec(memory_space=pl.ANY)
    return pl.pallas_call(
        pack_kernel,
        out_shape=(
            jax.ShapeDtypeStruct((DEVICES, DATA_TILES + 1, SUB, LANES), jnp.bfloat16),
            jax.ShapeDtypeStruct((1, ROWS), jnp.int32),
        ),
        in_specs=[hbm] * 3,
        out_specs=(hbm, hbm),
        scratch_shapes=[
            pltpu.VMEM((1, ROWS), jnp.int32),
            pltpu.VMEM((1, ROWS), jnp.int32),
            pltpu.VMEM((ROWS, WIDTH), jnp.bfloat16),
            pltpu.VMEM((DEVICES, DATA_TILES, SUB, LANES), jnp.bfloat16),
            pltpu.VMEM((DEVICES, SUB, LANES), jnp.bfloat16),
            pltpu.VMEM((1, ROWS), jnp.int32),
            pltpu.SemaphoreType.DMA((3,)),
            pltpu.SemaphoreType.DMA((2 + PARTS,)),
        ],
        compiler_params=pltpu.CompilerParams(vmem_limit_bytes=PACK_VMEM),
    )(ids, keep, embeddings)


def middle_kernel(arrived, centroids_hbm, products_hbm, centroids, products_ref, out_sem):
    flat = (DEVICES * SUB, LANES)
    codes = arrived[:, DATA_TILES].reshape(flat)
    place = (iota(flat, 0) >> 2) & (GROUP - 1) == iota(flat, 1) >> 3
    codes = jnp.where(place, codes.astype(jnp.float32), 0.0).astype(jnp.bfloat16)
    row, column = iota((CAP, DEVICES * SUB), 0), iota((CAP, DEVICES * SUB), 1)
    part = column & (SUB - 1)
    weight = jnp.where(part == 0, CODE_BASE, jnp.where(part == 1, 1, 0))
    weight = jnp.where(column >> 6 == row, weight, 0)
    code = matmul(weight.astype(jnp.float32).astype(jnp.bfloat16), codes).astype(jnp.int32)
    code = jnp.concatenate([code[k:k + 1] for k in range(CAP)], axis=1)
    keep_base = CODE_BASE * CODE_KEEP
    owner = (code & (keep_base - 1)) - CODE_BASE
    kept = jnp.where(code >= keep_base, owner, -1)
    rows = jnp.concatenate(
        [arrived[:, c * PER:(c + 1) * PER].reshape(SLOTS, LANES) for c in range(WIDTH // LANES)], axis=1
    )
    labels = iota((CLUSTER_PAD, SLOTS), 0)
    sums = matmul(as_bf16(labels == kept), rows)
    inv_scale = lax.rsqrt(
        jnp.sum(sums * sums, axis=1, keepdims=True) * (1.0 / WIDTH) + 1e-06
    ) / math.sqrt(WIDTH)
    unit = (sums * inv_scale).astype(jnp.bfloat16)
    centroids[...] = unit[:CLUSTER_DEV]
    stores = [pltpu.make_async_copy(centroids, centroids_hbm, out_sem.at[0])]
    stores[-1].start()
    similar = matmul(unit, rows, NT)
    products = jnp.sum(jnp.where(labels == owner, similar, 0.0), axis=0, keepdims=True)
    spread = jnp.concatenate(
        [jnp.broadcast_to(products[:, k * LANES:(k + 1) * LANES], (GROUP, LANES)) for k in range(CAP)], axis=0
    )
    square = (DEVICES, LANES)
    products_ref[...] = jnp.where(iota(square, 0) & (GROUP - 1) == iota(square, 1) >> 3, spread, 0.0)
    stores.append(pltpu.make_async_copy(products_ref, products_hbm, out_sem.at[1]))
    stores[-1].start()
    for store in stores:
        store.wait()


def middle(arrived):
    vmem = pl.BlockSpec(memory_space=pltpu.VMEM)
    hbm = pl.BlockSpec(memory_space=pl.ANY)
    return pl.pallas_call(
        middle_kernel,
        out_shape=(
            jax.ShapeDtypeStruct((CLUSTER_DEV, WIDTH), jnp.bfloat16),
            jax.ShapeDtypeStruct((DEVICES, LANES), jnp.float32),
        ),
        in_specs=[vmem],
        out_specs=(hbm, hbm),
        scratch_shapes=[
            pltpu.VMEM((CLUSTER_DEV, WIDTH), jnp.bfloat16),
            pltpu.VMEM((DEVICES, LANES), jnp.float32),
            pltpu.SemaphoreType.DMA((2,)),
        ],
        compiler_params=pltpu.CompilerParams(vmem_limit_bytes=VMEM_LIMIT),
    )(arrived)


def final_kernel(returned_ref, slot_ref, scale_ref, scores_ref):
    slot = slot_ref[...]
    hits = as_bf16(iota((DEVICES, ROWS), 0) == slot >> 3)
    back = jnp.sum(returned_ref[...].T.reshape(GROUP, CAP, DEVICES), axis=0)
    total = None
    for part in split3(back):
        term = matmul(part, hits)
        total = term if total is None else total + term
    chosen = jnp.where(iota((CAP, ROWS), 0) == slot & (CAP - 1), total, 0.0)
    scores_ref[...] = jnp.sum(chosen, axis=0, keepdims=True) * scale_ref[...]


def final(returned, slot, scale):
    vmem = pl.BlockSpec(memory_space=pltpu.VMEM)
    return pl.pallas_call(
        final_kernel,
        out_shape=jax.ShapeDtypeStruct((1, ROWS), jnp.float32),
        in_specs=[vmem] * 3,
        out_specs=vmem,
        compiler_params=pltpu.CompilerParams(vmem_limit_bytes=16 * 1024 * 1024),
    )(returned, slot, scale)


def body(embeddings, cluster_ids, keep_flags):
    outgoing, slot = pack(cluster_ids.reshape(1, ROWS), keep_flags.reshape(1, ROWS), embeddings)
    arrived = lax.all_to_all(outgoing, AXES, split_axis=0, concat_axis=0, tiled=True)
    row_scale = lax.rsqrt(
        jnp.mean(jnp.square(embeddings.astype(jnp.float32)), axis=1) + 1e-06
    ) / math.sqrt(WIDTH)
    centroids, products = middle(arrived)
    returned = lax.all_to_all(products, AXES, split_axis=0, concat_axis=0, tiled=True)
    scores = final(returned, slot, row_scale.reshape(1, ROWS))
    return (centroids, scores.reshape(ROWS))


def solution(mesh):
    in_specs = (P(AXES, None), P(AXES), P(AXES))
    out_specs = (P(AXES, None), P(AXES))
    return jax.shard_map(body, mesh=mesh, in_specs=in_specs, out_specs=out_specs, check_vma=False)
```

time: 62.8 us -> 59.9 us (0.954)
  Pallas kernels: 8.76 us -> 7.25 us
  waiting for transfers between devices: 37.1 us -> 35.7 us
    all_to_all x1, waiting for transfers between devices: 27.5 us -> 26.1 us  [body(): lax.all_to_all(outgoing, AXES, split_axis=0, concat_axis=0, tiled=True)]
    pallas_call x1, Pallas kernels: 4.49 us -> 3.3 us  [pack(): pl.pallas_call(pack_kernel, out_shape=(jax.ShapeDtypeStruct((DEVICES, DAT...]
where the time goes in v3:
time: 59.9 us; the launch traced here: 59.6 us
  waiting for transfers between devices  35.7 us (60%)
  starting transfers between devices  15.7 us (26%)
  Pallas kernels  7.25 us (12%)
  between operations  0.69 us (1%)
    all_to_all x1, waiting for transfers between devices, body(): lax.all_to_all(outgoing, AXES, split_axis=0, concat_axis=0, tiled=True)  26.1 us
    all_to_all x1, starting transfers between devices, body(): lax.all_to_all(outgoing, AXES, split_axis=0, concat_axis=0, tiled=True)  11.5 us
    all_to_all x1, waiting for transfers between devices, body(): lax.all_to_all(products, AXES, split_axis=0, concat_axis=0, tiled=True)  9.62 us
    all_to_all x1, starting transfers between devices, body(): lax.all_to_all(products, AXES, split_axis=0, concat_axis=0, tiled=True)  4.2 us
    pallas_call x1, Pallas kernels, pack(): pl.pallas_call(pack_kernel, out_shape=(jax.ShapeDtypeStruct((DEVICES, DAT...  3.3 us
    pallas_call x1, Pallas kernels, middle(): pl.pallas_call(middle_kernel, out_shape=(jax.ShapeDtypeStruct((CLUSTER_DE...  3.11 us
  transfers between devices with their start and end apart: 2, of which 2 were waited for; matrix products, arithmetic and copies ran while one was open for 0% of the time, Pallas kernels for 0%

profile of v3, /device:TPU:1, one launch (start us, length us, event | category | flops | bytes accessed | tf_op | source)
XLA Modules:
  0.0 59.6 jit_solution(6302264060511763837)
XLA Ops:
  0.6 3.3 %shard_map.50 = (bf16[128,13,4,128]{3,2,1,0:T(4,128)(2,1)}, s32[1,512]{1,0:T(1,128)}) custom-call(s32[1,512]{1,0:T(1,128)} %bitcast.10, s32[1,512]{1,0:T(1,128)} %bitcast.11, bf16[512,768]{1,0:T(8,128)(2,1)} %emb_hbm.1), custom_call_target="tpu_custom_call" | custom-call | tf_op jit(solution)/shard_map/pallas_call | solution.py:123
  3.9 0.0 copy-start.1
  3.9 11.5 %all-to-all-start = ((bf16[128,13,4,128]{3,2,1,0:T(4,128)(2,1)}), bf16[128,13,4,128]{3,2,1,0:T(4,128)(2,1)S(1)}, u32[]{:S(2)}, u32[]{:S(2)}) async-start(bf16[128,13,4,128]{3,2,1,0:T(4,128)(2,1)} %get-tuple-element.6), calls=%async_computation | async-start | bytes 3407872 | tf_op jit(solution)/shard_map/all_to_all | solution.py:229
  15.5 0.0 copy-done.1
  15.5 0.0 copy-start
  15.5 0.2 multiply_reduce_fusion
  15.7 26.1 %all-to-all-done.arrived = bf16[128,13,4,128]{3,2,1,0:T(4,128)(2,1)S(1)} async-done(((bf16[128,13,4,128]{3,2,1,0:T(4,128)(2,1)}), bf16[128,13,4,128]{3,2,1,0:T(4,128)(2,1)S(1)}, u32[]{:S(2)}, u32[]{:S(2)}) %all-to-all-start) | async-done | bytes 1703968 | tf_op jit(solution)/shard_map/all_to_all | solution.py:229
  41.8 3.1 %shard_map.51 = (bf16[392,768]{1,0:T(8,128)(2,1)}, f32[128,128]{1,0:T(8,128)}) custom-call(bf16[128,13,4,128]{3,2,1,0:T(4,128)(2,1)S(1)} %all-to-all-done.arrived), custom_call_target="tpu_custom_call" | custom-call | tf_op jit(solution)/shard_map/pallas_call | solution.py:187
  44.9 4.2 %all-to-all-start.1 = ((f32[128,1,128]{2,1,0:T(1,128)}), f32[128,1,128]{2,1,0:T(1,128)S(1)}, u32[]{:S(2)}, u32[]{:S(2)}) async-start(f32[128,1,128]{2,1,0:T(1,128)} %bitcast.3), calls=%async_computation.1 | async-start | bytes 131072 | tf_op jit(solution)/shard_map/all_to_all | solution.py:234
  49.2 9.6 %all-to-all-done.1 = f32[128,1,128]{2,1,0:T(1,128)S(1)} async-done(((f32[128,1,128]{2,1,0:T(1,128)}), f32[128,1,128]{2,1,0:T(1,128)S(1)}, u32[]{:S(2)}, u32[]{:S(2)}) %all-to-all-start.1) | async-done | bytes 65568 | tf_op jit(solution)/shard_map/all_to_all | solution.py:234
  58.8 0.0 copy-done
  58.8 0.8 %shard_map.52 = f32[1,512]{1,0:T(1,128)} custom-call(f32[128,128]{1,0:T(8,128)S(1)} %bitcast.8, s32[1,512]{1,0:T(1,128)S(1)} %copy-done, f32[1,512]{1,0:T(1,128)S(1)} %bitcast.9), custom_call_target="tpu_custom_call" | custom-call | tf_op jit(solution)/shard_map/pallas_call | solution.py:218
  (1 shorter events, 0.0 us)
Async XLA Ops:
  3.9 11.5 %copy-start.1 = (bf16[512,768]{1,0:T(8,128)(2,1)S(1)}, bf16[512,768]{1,0:T(8,128)(2,1)}, u32[]{:S(2)}) copy-start(bf16[512,768]{1,0:T(8,128)(2,1)} %emb_hbm.1) | copy-start | bytes 2359300
  3.9 37.9 %all-to-all-start = ((bf16[128,13,4,128]{3,2,1,0:T(4,128)(2,1)}), bf16[128,13,4,128]{3,2,1,0:T(4,128)(2,1)S(1)}, u32[]{:S(2)}, u32[]{:S(2)}) async-start(bf16[128,13,4,128]{3,2,1,0:T(4,128)(2,1)} %get-tuple-element.6), calls=%async_computation | async-start | bytes 3407872 | tf_op jit(solution)/shard_map/all_to_all | solution.py:229
  15.5 43.3 %copy-start = (s32[1,512]{1,0:T(1,128)S(1)}, s32[1,512]{1,0:T(1,128)}, u32[]{:S(2)}) copy-start(s32[1,512]{1,0:T(1,128)} %get-tuple-element.9.slot_ref) | copy-start | bytes 6148
  44.9 13.8 %all-to-all-start.1 = ((f32[128,1,128]{2,1,0:T(1,128)}), f32[128,1,128]{2,1,0:T(1,128)S(1)}, u32[]{:S(2)}, u32[]{:S(2)}) async-start(f32[128,1,128]{2,1,0:T(1,128)} %bitcast.3), calls=%async_computation.1 | async-start | bytes 131072 | tf_op jit(solution)/shard_map/all_to_all | solution.py:234

commit v4 on v3

--- a/solution.py
+++ b/solution.py
@@ -9,7 +9,7 @@
 
 AXES = ("doc", "own")
 CLUSTER_DEV = 392
-CLUSTER_PAD = 400
+CHUNKS = ((0, 208, 208), (208, 192, 184))
 DEVICES = 128
 CAP = 8
 SLOTS = DEVICES * CAP
@@ -22,9 +22,7 @@
 GROUP = LANES // CAP
 CODE_BASE = 16
 CODE_KEEP = 32
-PARTS = 4
-PART = SLOTS // PARTS
-PART_PEERS = DEVICES // PARTS
+PARTS = (256, 256, 256, 128, 128)
 PACK_VMEM = 63 * 1024 * 1024
 VMEM_LIMIT = 48 * 1024 * 1024
 
@@ -103,17 +101,19 @@
     stores.append(pltpu.make_async_copy(codes, out_hbm.at[:, DATA_TILES], out_sem.at[1]))
     stores[-1].start()
     loads[2].wait()
-    for k in range(PARTS):
-        place = as_bf16(iota((PART, ROWS), 0) + k * PART == slot)
+    first = 0
+    for k, count in enumerate(PARTS):
+        place = as_bf16(iota((count, ROWS), 0) + first == slot)
         block = matmul(place, emb[...]).astype(jnp.bfloat16)
-        peers = pl.ds(k * PART_PEERS, PART_PEERS)
+        peers = pl.ds(first // CAP, count // CAP)
         for c in range(WIDTH // LANES):
-            piece = block[:, c * LANES:(c + 1) * LANES].reshape(PART_PEERS, PER, SUB, LANES)
+            piece = block[:, c * LANES:(c + 1) * LANES].reshape(count // CAP, PER, SUB, LANES)
             staged[peers, c * PER:(c + 1) * PER] = piece
         stores.append(
             pltpu.make_async_copy(staged.at[peers], out_hbm.at[peers, pl.ds(0, DATA_TILES)], out_sem.at[2 + k])
         )
         stores[-1].start()
+        first += count
     for store in stores:
         store.wait()
 
@@ -136,7 +136,7 @@
             pltpu.VMEM((DEVICES, SUB, LANES), jnp.bfloat16),
             pltpu.VMEM((1, ROWS), jnp.int32),
             pltpu.SemaphoreType.DMA((3,)),
-            pltpu.SemaphoreType.DMA((2 + PARTS,)),
+            pltpu.SemaphoreType.DMA((2 + len(PARTS),)),
         ],
         compiler_params=pltpu.CompilerParams(vmem_limit_bytes=PACK_VMEM),
     )(ids, keep, embeddings)
@@ -159,23 +159,27 @@
     rows = jnp.concatenate(
         [arrived[:, c * PER:(c + 1) * PER].reshape(SLOTS, LANES) for c in range(WIDTH // LANES)], axis=1
     )
-    labels = iota((CLUSTER_PAD, SLOTS), 0)
-    sums = matmul(as_bf16(labels == kept), rows)
-    inv_scale = lax.rsqrt(
-        jnp.sum(sums * sums, axis=1, keepdims=True) * (1.0 / WIDTH) + 1e-06
-    ) / math.sqrt(WIDTH)
-    unit = (sums * inv_scale).astype(jnp.bfloat16)
-    centroids[...] = unit[:CLUSTER_DEV]
-    stores = [pltpu.make_async_copy(centroids, centroids_hbm, out_sem.at[0])]
-    stores[-1].start()
-    similar = matmul(unit, rows, NT)
-    products = jnp.sum(jnp.where(labels == owner, similar, 0.0), axis=0, keepdims=True)
+    labels = [iota((count, SLOTS), 0) + start for start, count, _ in CHUNKS]
+    sums = [matmul(as_bf16(label == kept), rows) for label in labels]
+    stores, products = [], None
+    for k, (start, _, real) in enumerate(CHUNKS):
+        inv_scale = lax.rsqrt(
+            jnp.sum(sums[k] * sums[k], axis=1, keepdims=True) * (1.0 / WIDTH) + 1e-06
+        ) / math.sqrt(WIDTH)
+        unit = (sums[k] * inv_scale).astype(jnp.bfloat16)
+        here = pl.ds(start, real)
+        centroids[here] = unit[:real]
+        stores.append(pltpu.make_async_copy(centroids.at[here], centroids_hbm.at[here], out_sem.at[k]))
+        stores[-1].start()
+        similar = matmul(unit, rows, NT)
+        part = jnp.sum(jnp.where(labels[k] == owner, similar, 0.0), axis=0, keepdims=True)
+        products = part if products is None else products + part
     spread = jnp.concatenate(
         [jnp.broadcast_to(products[:, k * LANES:(k + 1) * LANES], (GROUP, LANES)) for k in range(CAP)], axis=0
     )
     square = (DEVICES, LANES)
     products_ref[...] = jnp.where(iota(square, 0) & (GROUP - 1) == iota(square, 1) >> 3, spread, 0.0)
-    stores.append(pltpu.make_async_copy(products_ref, products_hbm, out_sem.at[1]))
+    stores.append(pltpu.make_async_copy(products_ref, products_hbm, out_sem.at[len(CHUNKS)]))
     stores[-1].start()
     for store in stores:
         store.wait()
@@ -195,7 +199,7 @@
         scratch_shapes=[
             pltpu.VMEM((CLUSTER_DEV, WIDTH), jnp.bfloat16),
             pltpu.VMEM((DEVICES, LANES), jnp.float32),
-            pltpu.SemaphoreType.DMA((2,)),
+            pltpu.SemaphoreType.DMA((len(CHUNKS) + 1,)),
         ],
         compiler_params=pltpu.CompilerParams(vmem_limit_bytes=VMEM_LIMIT),
     )(arrived)

time: 59.9 us -> 59.2 us (0.988)
  Pallas kernels: 7.25 us -> 6.63 us
where the time goes in v4:
time: 59.2 us; the launch traced here: 59 us
  waiting for transfers between devices  35.7 us (60%)
  starting transfers between devices  15.7 us (27%)
  Pallas kernels  6.63 us (11%)
  between operations  0.69 us (1%)
    all_to_all x1, waiting for transfers between devices, body(): lax.all_to_all(outgoing, AXES, split_axis=0, concat_axis=0, tiled=True)  26.1 us
    all_to_all x1, starting transfers between devices, body(): lax.all_to_all(outgoing, AXES, split_axis=0, concat_axis=0, tiled=True)  11.5 us
    all_to_all x1, waiting for transfers between devices, body(): lax.all_to_all(products, AXES, split_axis=0, concat_axis=0, tiled=True)  9.62 us
    all_to_all x1, starting transfers between devices, body(): lax.all_to_all(products, AXES, split_axis=0, concat_axis=0, tiled=True)  4.21 us
    pallas_call x1, Pallas kernels, pack(): pl.pallas_call(pack_kernel, out_shape=(jax.ShapeDtypeStruct((DEVICES, DAT...  3.22 us
    pallas_call x1, Pallas kernels, middle(): pl.pallas_call(middle_kernel, out_shape=(jax.ShapeDtypeStruct((CLUSTER_DE...  2.56 us
  transfers between devices with their start and end apart: 2, of which 2 were waited for; matrix products, arithmetic and copies ran while one was open for 0% of the time, Pallas kernels for 0%

profile of v4, /device:TPU:1, one launch (start us, length us, event | category | flops | bytes accessed | tf_op | source)
XLA Modules:
  0.0 59.0 jit_solution(7125922735117364470)
XLA Ops:
  0.6 3.2 %shard_map.50 = (bf16[128,13,4,128]{3,2,1,0:T(4,128)(2,1)}, s32[1,512]{1,0:T(1,128)}) custom-call(s32[1,512]{1,0:T(1,128)} %bitcast.10, s32[1,512]{1,0:T(1,128)} %bitcast.11, bf16[512,768]{1,0:T(8,128)(2,1)} %emb_hbm.1), custom_call_target="tpu_custom_call" | custom-call | tf_op jit(solution)/shard_map/pallas_call | solution.py:123
  3.9 0.0 copy-start.1
  3.9 11.5 %all-to-all-start = ((bf16[128,13,4,128]{3,2,1,0:T(4,128)(2,1)}), bf16[128,13,4,128]{3,2,1,0:T(4,128)(2,1)S(1)}, u32[]{:S(2)}, u32[]{:S(2)}) async-start(bf16[128,13,4,128]{3,2,1,0:T(4,128)(2,1)} %get-tuple-element.6), calls=%async_computation | async-start | bytes 3407872 | tf_op jit(solution)/shard_map/all_to_all | solution.py:233
  15.4 0.0 copy-done.1
  15.4 0.0 copy-start
  15.4 0.2 multiply_reduce_fusion
  15.6 26.1 %all-to-all-done.arrived = bf16[128,13,4,128]{3,2,1,0:T(4,128)(2,1)S(1)} async-done(((bf16[128,13,4,128]{3,2,1,0:T(4,128)(2,1)}), bf16[128,13,4,128]{3,2,1,0:T(4,128)(2,1)S(1)}, u32[]{:S(2)}, u32[]{:S(2)}) %all-to-all-start) | async-done | bytes 1703968 | tf_op jit(solution)/shard_map/all_to_all | solution.py:233
  41.7 2.6 %shard_map.51 = (bf16[392,768]{1,0:T(8,128)(2,1)}, f32[128,128]{1,0:T(8,128)}) custom-call(bf16[128,13,4,128]{3,2,1,0:T(4,128)(2,1)S(1)} %all-to-all-done.arrived), custom_call_target="tpu_custom_call" | custom-call | tf_op jit(solution)/shard_map/pallas_call | solution.py:191
  44.3 4.2 %all-to-all-start.1 = ((f32[128,1,128]{2,1,0:T(1,128)}), f32[128,1,128]{2,1,0:T(1,128)S(1)}, u32[]{:S(2)}, u32[]{:S(2)}) async-start(f32[128,1,128]{2,1,0:T(1,128)} %bitcast.3), calls=%async_computation.1 | async-start | bytes 131072 | tf_op jit(solution)/shard_map/all_to_all | solution.py:238
  48.6 9.6 %all-to-all-done.1 = f32[128,1,128]{2,1,0:T(1,128)S(1)} async-done(((f32[128,1,128]{2,1,0:T(1,128)}), f32[128,1,128]{2,1,0:T(1,128)S(1)}, u32[]{:S(2)}, u32[]{:S(2)}) %all-to-all-start.1) | async-done | bytes 65568 | tf_op jit(solution)/shard_map/all_to_all | solution.py:238
  58.2 0.0 copy-done
  58.2 0.8 %shard_map.52 = f32[1,512]{1,0:T(1,128)} custom-call(f32[128,128]{1,0:T(8,128)S(1)} %bitcast.8, s32[1,512]{1,0:T(1,128)S(1)} %copy-done, f32[1,512]{1,0:T(1,128)S(1)} %bitcast.9), custom_call_target="tpu_custom_call" | custom-call | tf_op jit(solution)/shard_map/pallas_call | solution.py:222
  (1 shorter events, 0.0 us)
Async XLA Ops:
  3.9 11.5 %copy-start.1 = (bf16[512,768]{1,0:T(8,128)(2,1)S(1)}, bf16[512,768]{1,0:T(8,128)(2,1)}, u32[]{:S(2)}) copy-start(bf16[512,768]{1,0:T(8,128)(2,1)} %emb_hbm.1) | copy-start | bytes 2359300
  3.9 37.9 %all-to-all-start = ((bf16[128,13,4,128]{3,2,1,0:T(4,128)(2,1)}), bf16[128,13,4,128]{3,2,1,0:T(4,128)(2,1)S(1)}, u32[]{:S(2)}, u32[]{:S(2)}) async-start(bf16[128,13,4,128]{3,2,1,0:T(4,128)(2,1)} %get-tuple-element.6), calls=%async_computation | async-start | bytes 3407872 | tf_op jit(solution)/shard_map/all_to_all | solution.py:233
  15.4 42.8 %copy-start = (s32[1,512]{1,0:T(1,128)S(1)}, s32[1,512]{1,0:T(1,128)}, u32[]{:S(2)}) copy-start(s32[1,512]{1,0:T(1,128)} %get-tuple-element.9.slot_ref) | copy-start | bytes 6148
  44.3 13.9 %all-to-all-start.1 = ((f32[128,1,128]{2,1,0:T(1,128)}), f32[128,1,128]{2,1,0:T(1,128)S(1)}, u32[]{:S(2)}, u32[]{:S(2)}) async-start(f32[128,1,128]{2,1,0:T(1,128)} %bitcast.3), calls=%async_computation.1 | async-start | bytes 131072 | tf_op jit(solution)/shard_map/all_to_all | solution.py:238

commit v5 on v4

--- a/solution.py
+++ b/solution.py
@@ -104,11 +104,11 @@
     first = 0
     for k, count in enumerate(PARTS):
         place = as_bf16(iota((count, ROWS), 0) + first == slot)
-        block = matmul(place, emb[...]).astype(jnp.bfloat16)
+        block = matmul(place, emb[...])
         peers = pl.ds(first // CAP, count // CAP)
         for c in range(WIDTH // LANES):
             piece = block[:, c * LANES:(c + 1) * LANES].reshape(count // CAP, PER, SUB, LANES)
-            staged[peers, c * PER:(c + 1) * PER] = piece
+            staged[peers, c * PER:(c + 1) * PER] = piece.astype(jnp.bfloat16)
         stores.append(
             pltpu.make_async_copy(staged.at[peers], out_hbm.at[peers, pl.ds(0, DATA_TILES)], out_sem.at[2 + k])
         )
@@ -142,7 +142,11 @@
     )(ids, keep, embeddings)
 
 
-def middle_kernel(arrived, centroids_hbm, products_hbm, centroids, products_ref, out_sem):
+def middle_kernel(
+    arrived, emb_hbm, centroids_hbm, products_hbm, scale_ref, emb, centroids, products_ref, in_sem, out_sem
+):
+    load = pltpu.make_async_copy(emb_hbm, emb, in_sem)
+    load.start()
     flat = (DEVICES * SUB, LANES)
     codes = arrived[:, DATA_TILES].reshape(flat)
     place = (iota(flat, 0) >> 2) & (GROUP - 1) == iota(flat, 1) >> 3
@@ -167,10 +171,10 @@
             jnp.sum(sums[k] * sums[k], axis=1, keepdims=True) * (1.0 / WIDTH) + 1e-06
         ) / math.sqrt(WIDTH)
         unit = (sums[k] * inv_scale).astype(jnp.bfloat16)
-        here = pl.ds(start, real)
-        centroids[here] = unit[:real]
-        stores.append(pltpu.make_async_copy(centroids.at[here], centroids_hbm.at[here], out_sem.at[k]))
-        stores[-1].start()
+        centroids[pl.ds(start, real)] = unit[:real]
+        if k == len(CHUNKS) - 1:
+            stores.append(pltpu.make_async_copy(centroids, centroids_hbm, out_sem.at[0]))
+            stores[-1].start()
         similar = matmul(unit, rows, NT)
         part = jnp.sum(jnp.where(labels[k] == owner, similar, 0.0), axis=0, keepdims=True)
         products = part if products is None else products + part
@@ -179,13 +183,20 @@
     )
     square = (DEVICES, LANES)
     products_ref[...] = jnp.where(iota(square, 0) & (GROUP - 1) == iota(square, 1) >> 3, spread, 0.0)
-    stores.append(pltpu.make_async_copy(products_ref, products_hbm, out_sem.at[len(CHUNKS)]))
+    stores.append(pltpu.make_async_copy(products_ref, products_hbm, out_sem.at[1]))
     stores[-1].start()
+    load.wait()
+    total = None
+    for c in range(WIDTH // LANES):
+        piece = emb[:, c * LANES:(c + 1) * LANES].astype(jnp.float32)
+        total = piece * piece if total is None else total + piece * piece
+    squares = jnp.sum(total.T, axis=0, keepdims=True)
+    scale_ref[...] = lax.rsqrt(squares * (1.0 / WIDTH) + 1e-06) / math.sqrt(WIDTH)
     for store in stores:
         store.wait()
 
 
-def middle(arrived):
+def middle(arrived, embeddings):
     vmem = pl.BlockSpec(memory_space=pltpu.VMEM)
     hbm = pl.BlockSpec(memory_space=pl.ANY)
     return pl.pallas_call(
@@ -193,16 +204,19 @@
         out_shape=(
             jax.ShapeDtypeStruct((CLUSTER_DEV, WIDTH), jnp.bfloat16),
             jax.ShapeDtypeStruct((DEVICES, LANES), jnp.float32),
+            jax.ShapeDtypeStruct((1, ROWS), jnp.float32),
         ),
-        in_specs=[vmem],
-        out_specs=(hbm, hbm),
+        in_specs=[vmem, hbm],
+        out_specs=(hbm, hbm, vmem),
         scratch_shapes=[
+            pltpu.VMEM((ROWS, WIDTH), jnp.bfloat16),
             pltpu.VMEM((CLUSTER_DEV, WIDTH), jnp.bfloat16),
             pltpu.VMEM((DEVICES, LANES), jnp.float32),
-            pltpu.SemaphoreType.DMA((len(CHUNKS) + 1,)),
+            pltpu.SemaphoreType.DMA,
+            pltpu.SemaphoreType.DMA((2,)),
         ],
         compiler_params=pltpu.CompilerParams(vmem_limit_bytes=VMEM_LIMIT),
-    )(arrived)
+    )(arrived, embeddings)
 
 
 def final_kernel(returned_ref, slot_ref, scale_ref, scores_ref):
@@ -231,12 +245,9 @@
 def body(embeddings, cluster_ids, keep_flags):
     outgoing, slot = pack(cluster_ids.reshape(1, ROWS), keep_flags.reshape(1, ROWS), embeddings)
     arrived = lax.all_to_all(outgoing, AXES, split_axis=0, concat_axis=0, tiled=True)
-    row_scale = lax.rsqrt(
-        jnp.mean(jnp.square(embeddings.astype(jnp.float32)), axis=1) + 1e-06
-    ) / math.sqrt(WIDTH)
-    centroids, products = middle(arrived)
+    centroids, products, row_scale = middle(arrived, embeddings)
     returned = lax.all_to_all(products, AXES, split_axis=0, concat_axis=0, tiled=True)
-    scores = final(returned, slot, row_scale.reshape(1, ROWS))
+    scores = final(returned, slot, row_scale)
     return (centroids, scores.reshape(ROWS))
 
 

time: 59.2 us -> 58.5 us (0.988)
  blocking collectives: 0 us -> 51.4 us
  waiting for transfers between devices: 35.7 us -> 0 us
  starting transfers between devices: 15.7 us -> 0 us
    all_to_all x0 -> x2, blocking collectives: none -> 51.4 us  [the longest x1 37.9 us: body(): lax.all_to_all(outgoing, AXES, split_axis=0, concat_axis=0, tiled=True)]
    all_to_all x2 -> x0, waiting for transfers between devices: 35.7 us -> none  [the longest x1 26.1 us: body(): lax.all_to_all(outgoing, AXES, split_axis=0, concat_axis=0, tiled=True)]
    all_to_all x2 -> x0, starting transfers between devices: 15.7 us -> none  [the longest x1 11.5 us: body(): lax.all_to_all(outgoing, AXES, split_axis=0, concat_axis=0, tiled=True)]
  transfers between devices with their start and end apart: 2 -> 0, of which waited for: 2 -> 0; matrix products, arithmetic and copies ran while one was open for 0% -> 0% of each run, Pallas kernels for 0% -> 0%
where the time goes in v5:
time: 58.5 us; the launch traced here: 58.3 us
  blocking collectives  51.4 us (88%)
  Pallas kernels  6.28 us (11%)
  between operations  0.66 us (1%)
    all_to_all x1, blocking collectives, body(): lax.all_to_all(outgoing, AXES, split_axis=0, concat_axis=0, tiled=True)  37.9 us
    all_to_all x1, blocking collectives, body(): lax.all_to_all(products, AXES, split_axis=0, concat_axis=0, tiled=True)  13.5 us
    pallas_call x1, Pallas kernels, pack(): pl.pallas_call(pack_kernel, out_shape=(jax.ShapeDtypeStruct((DEVICES, DAT...  3.13 us
    pallas_call x1, Pallas kernels, middle(): pl.pallas_call(middle_kernel, out_shape=(jax.ShapeDtypeStruct((CLUSTER_DE...  2.3 us

profile of v5, /device:TPU:1, one launch (start us, length us, event | category | flops | bytes accessed | tf_op | source)
XLA Modules:
  0.0 58.3 jit_solution(5885399307560476019)
XLA Ops:
  0.6 3.1 %shard_map.50 = (bf16[128,13,4,128]{3,2,1,0:T(4,128)(2,1)}, s32[1,512]{1,0:T(1,128)}) custom-call(s32[1,512]{1,0:T(1,128)} %bitcast.9, s32[1,512]{1,0:T(1,128)} %bitcast.10, bf16[512,768]{1,0:T(8,128)(2,1)} %emb_hbm.3), custom_call_target="tpu_custom_call" | custom-call | tf_op jit(solution)/shard_map/pallas_call | solution.py:123
  3.8 0.0 copy-start
  3.8 37.9 %all_to_all.16.arrived = bf16[128,13,4,128]{3,2,1,0:T(4,128)(2,1)S(1)} all-to-all(bf16[128,13,4,128]{3,2,1,0:T(4,128)(2,1)} %get-tuple-element.7), channel_id=1, replica_groups=mesh['doc'=16,'own'=8] {'doc','own'}, dimensions={0} | all-to-all | bytes 3407872 | tf_op jit(solution)/shard_map/all_to_all | solution.py:247
  41.7 0.0 copy-done
  41.7 0.0 copy-start.1
  41.7 2.3 %shard_map.51 = (bf16[392,768]{1,0:T(8,128)(2,1)}, f32[128,128]{1,0:T(8,128)S(1)}, f32[1,512]{1,0:T(1,128)S(1)}) custom-call(bf16[128,13,4,128]{3,2,1,0:T(4,128)(2,1)S(1)} %all_to_all.16.arrived, bf16[512,768]{1,0:T(8,128)(2,1)S(1)} %copy-done), custom_call_target="tpu_custom_call" | custom-call | tf_op jit(solution)/shard_map/pallas_call | solution.py:202
  44.0 13.5 %all_to_all.17 = f32[128,1,128]{2,1,0:T(1,128)S(1)} all-to-all(f32[128,1,128]{2,1,0:T(1,128)S(1)} %bitcast.8), channel_id=1, replica_groups=mesh['doc'=16,'own'=8] {'doc','own'}, dimensions={0} | all-to-all | bytes 131072 | tf_op jit(solution)/shard_map/all_to_all | solution.py:249
  57.5 0.0 copy-done.1
  57.5 0.8 %shard_map.52 = f32[1,512]{1,0:T(1,128)} custom-call(f32[128,128]{1,0:T(8,128)S(1)} %bitcast.7, s32[1,512]{1,0:T(1,128)S(1)} %copy-done.1, f32[1,512]{1,0:T(1,128)S(1)} %get-tuple-element.11.scale_ref), custom_call_target="tpu_custom_call" | custom-call | tf_op jit(solution)/shard_map/pallas_call | solution.py:236
Async XLA Ops:
  3.8 37.9 %copy-start = (bf16[512,768]{1,0:T(8,128)(2,1)S(1)}, bf16[512,768]{1,0:T(8,128)(2,1)}, u32[]{:S(2)}) copy-start(bf16[512,768]{1,0:T(8,128)(2,1)} %emb_hbm.3) | copy-start | bytes 2359300
  41.7 15.8 %copy-start.1 = (s32[1,512]{1,0:T(1,128)S(1)}, s32[1,512]{1,0:T(1,128)}, u32[]{:S(2)}) copy-start(s32[1,512]{1,0:T(1,128)} %get-tuple-element.10.slot_ref) | copy-start | bytes 6148

commit v6 on v5

--- a/solution.py
+++ b/solution.py
@@ -23,7 +23,7 @@
 CODE_BASE = 16
 CODE_KEEP = 32
 PARTS = (256, 256, 256, 128, 128)
-PACK_VMEM = 63 * 1024 * 1024
+PACK_VMEM = 40 * 1024 * 1024
 VMEM_LIMIT = 48 * 1024 * 1024
 
 NN = (((1,), (0,)), ((), ()))
@@ -55,7 +55,7 @@
 
 
 def pack_kernel(
-    ids_hbm, keep_hbm, emb_hbm, out_hbm, slot_hbm, ids_ref, keep_ref, emb, staged, codes, slots, in_sem, out_sem
+    ids_hbm, keep_hbm, emb_hbm, out_ref, slot_ref, ids_ref, keep_ref, emb, in_sem
 ):
     loads = [
         pltpu.make_async_copy(source, kept, in_sem.at[k])
@@ -84,9 +84,7 @@
     counts = jnp.concatenate(before, axis=1)
     position = jnp.sum(jnp.where(hits, counts, 0.0), axis=0, keepdims=True).astype(jnp.int32)
     slot = target * CAP + position
-    slots[...] = slot
-    stores = [pltpu.make_async_copy(slots, slot_hbm, out_sem.at[0])]
-    stores[-1].start()
+    slot_ref[...] = slot
     at_slot = iota((LANES, ROWS), 0) & (CAP - 1) == position
     upper = (local >> 4) + 1 + CODE_KEEP * keep_ref[...]
     lower = local & (CODE_BASE - 1)
@@ -97,9 +95,7 @@
     which = iota((DEVICES, SUB, LANES), 1)
     tile = jnp.where(which == 1, coded[1][:, None, :], 0.0)
     tile = jnp.where(which == 0, coded[0][:, None, :], tile)
-    codes[...] = tile.astype(jnp.bfloat16)
-    stores.append(pltpu.make_async_copy(codes, out_hbm.at[:, DATA_TILES], out_sem.at[1]))
-    stores[-1].start()
+    out_ref[:, DATA_TILES] = tile.astype(jnp.bfloat16)
     loads[2].wait()
     first = 0
     for k, count in enumerate(PARTS):
@@ -108,18 +104,14 @@
         peers = pl.ds(first // CAP, count // CAP)
         for c in range(WIDTH // LANES):
             piece = block[:, c * LANES:(c + 1) * LANES].reshape(count // CAP, PER, SUB, LANES)
-            staged[peers, c * PER:(c + 1) * PER] = piece.astype(jnp.bfloat16)
-        stores.append(
-            pltpu.make_async_copy(staged.at[peers], out_hbm.at[peers, pl.ds(0, DATA_TILES)], out_sem.at[2 + k])
-        )
-        stores[-1].start()
+            out_ref[peers, c * PER:(c + 1) * PER] = piece.astype(jnp.bfloat16)
         first += count
-    for store in stores:
-        store.wait()
 
 
 def pack(ids, keep, embeddings):
+    vmem = pl.BlockSpec(memory_space=pltpu.VMEM)
     hbm = pl.BlockSpec(memory_space=pl.ANY)
+    operands = [pltpu.with_memory_space_constraint(x, pltpu.HBM) for x in (ids, keep, embeddings)]
     return pl.pallas_call(
         pack_kernel,
         out_shape=(
@@ -127,19 +119,15 @@
             jax.ShapeDtypeStruct((1, ROWS), jnp.int32),
         ),
         in_specs=[hbm] * 3,
-        out_specs=(hbm, hbm),
+        out_specs=(vmem, vmem),
         scratch_shapes=[
             pltpu.VMEM((1, ROWS), jnp.int32),
             pltpu.VMEM((1, ROWS), jnp.int32),
             pltpu.VMEM((ROWS, WIDTH), jnp.bfloat16),
-            pltpu.VMEM((DEVICES, DATA_TILES, SUB, LANES), jnp.bfloat16),
-            pltpu.VMEM((DEVICES, SUB, LANES), jnp.bfloat16),
-            pltpu.VMEM((1, ROWS), jnp.int32),
             pltpu.SemaphoreType.DMA((3,)),
-            pltpu.SemaphoreType.DMA((2 + len(PARTS),)),
         ],
         compiler_params=pltpu.CompilerParams(vmem_limit_bytes=PACK_VMEM),
-    )(ids, keep, embeddings)
+    )(*operands)
 
 
 def middle_kernel(

time: 58.5 us -> 57.4 us (0.981)
  Pallas kernels: 6.28 us -> 5.43 us
    pallas_call x1, Pallas kernels: 3.13 us -> 2.31 us  [pack(): pl.pallas_call(pack_kernel, out_shape=(jax.ShapeDtypeStruct((DEVICES, DAT...]
where the time goes in v6:
time: 57.4 us; the launch traced here: 57.3 us
  blocking collectives  51.2 us (89%)
  Pallas kernels  5.43 us (9%)
  between operations  0.66 us (1%)
    all_to_all x1, blocking collectives, body(): lax.all_to_all(outgoing, AXES, split_axis=0, concat_axis=0, tiled=True)  37.7 us
    all_to_all x1, blocking collectives, body(): lax.all_to_all(products, AXES, split_axis=0, concat_axis=0, tiled=True)  13.5 us
    pallas_call x1, Pallas kernels, pack(): pl.pallas_call(pack_kernel, out_shape=(jax.ShapeDtypeStruct((DEVICES, DAT...  2.31 us
    pallas_call x1, Pallas kernels, middle(): pl.pallas_call(middle_kernel, out_shape=(jax.ShapeDtypeStruct((CLUSTER_DE...  2.27 us

profile of v6, /device:TPU:1, one launch (start us, length us, event | category | flops | bytes accessed | tf_op | source)
XLA Modules:
  0.0 57.3 jit_solution(2650934094322858793)
XLA Ops:
  0.6 2.3 %shard_map.50 = (bf16[128,13,4,128]{3,2,1,0:T(4,128)(2,1)S(1)}, s32[1,512]{1,0:T(1,128)S(1)}) custom-call(s32[1,512]{1,0:T(1,128)} %bitcast.9, s32[1,512]{1,0:T(1,128)} %bitcast.10, bf16[512,768]{1,0:T(8,128)(2,1)} %emb_hbm.3), custom_call_target="tpu_custom_call" | custom-call | tf_op jit(solution)/shard_map/pallas_call | solution.py:115
  2.9 0.0 copy-start
  3.0 37.7 %all_to_all.16.arrived = bf16[128,13,4,128]{3,2,1,0:T(4,128)(2,1)S(1)} all-to-all(bf16[128,13,4,128]{3,2,1,0:T(4,128)(2,1)S(1)} %get-tuple-element.7), channel_id=1, replica_groups=mesh['doc'=16,'own'=8] {'doc','own'}, dimensions={0} | all-to-all | bytes 3407872 | tf_op jit(solution)/shard_map/all_to_all | solution.py:235
  40.6 0.0 copy-done
  40.6 2.3 %shard_map.51 = (bf16[392,768]{1,0:T(8,128)(2,1)}, f32[128,128]{1,0:T(8,128)S(1)}, f32[1,512]{1,0:T(1,128)S(1)}) custom-call(bf16[128,13,4,128]{3,2,1,0:T(4,128)(2,1)S(1)} %all_to_all.16.arrived, bf16[512,768]{1,0:T(8,128)(2,1)S(1)} %copy-done), custom_call_target="tpu_custom_call" | custom-call | tf_op jit(solution)/shard_map/pallas_call | solution.py:190
  42.9 13.5 %all_to_all.17 = f32[128,1,128]{2,1,0:T(1,128)S(1)} all-to-all(f32[128,1,128]{2,1,0:T(1,128)S(1)} %bitcast.8), channel_id=1, replica_groups=mesh['doc'=16,'own'=8] {'doc','own'}, dimensions={0} | all-to-all | bytes 131072 | tf_op jit(solution)/shard_map/all_to_all | solution.py:237
  56.4 0.8 %shard_map.52 = f32[1,512]{1,0:T(1,128)} custom-call(f32[128,128]{1,0:T(8,128)S(1)} %bitcast.7, s32[1,512]{1,0:T(1,128)S(1)} %get-tuple-element.10.slot_ref, f32[1,512]{1,0:T(1,128)S(1)} %get-tuple-element.11.scale_ref), custom_call_target="tpu_custom_call" | custom-call | tf_op jit(solution)/shard_map/pallas_call | solution.py:224
Async XLA Ops:
  2.9 37.7 %copy-start = (bf16[512,768]{1,0:T(8,128)(2,1)S(1)}, bf16[512,768]{1,0:T(8,128)(2,1)}, u32[]{:S(2)}) copy-start(bf16[512,768]{1,0:T(8,128)(2,1)} %emb_hbm.3) | copy-start | bytes 2359300

commit v7 on v6

--- a/solution.py
+++ b/solution.py
@@ -22,7 +22,7 @@
 GROUP = LANES // CAP
 CODE_BASE = 16
 CODE_KEEP = 32
-PARTS = (256, 256, 256, 128, 128)
+PARTS = (256, 256, 256, 256)
 PACK_VMEM = 40 * 1024 * 1024
 VMEM_LIMIT = 48 * 1024 * 1024
 
@@ -131,10 +131,8 @@
 
 
 def middle_kernel(
-    arrived, emb_hbm, centroids_hbm, products_hbm, scale_ref, emb, centroids, products_ref, in_sem, out_sem
+    arrived, emb, centroids_ref, products_ref, scale_ref
 ):
-    load = pltpu.make_async_copy(emb_hbm, emb, in_sem)
-    load.start()
     flat = (DEVICES * SUB, LANES)
     codes = arrived[:, DATA_TILES].reshape(flat)
     place = (iota(flat, 0) >> 2) & (GROUP - 1) == iota(flat, 1) >> 3
@@ -153,16 +151,19 @@
     )
     labels = [iota((count, SLOTS), 0) + start for start, count, _ in CHUNKS]
     sums = [matmul(as_bf16(label == kept), rows) for label in labels]
-    stores, products = [], None
+    total = None
+    for c in range(WIDTH // LANES):
+        piece = emb[:, c * LANES:(c + 1) * LANES].astype(jnp.float32)
+        total = piece * piece if total is None else total + piece * piece
+    squares = jnp.sum(total.T, axis=0, keepdims=True)
+    scale_ref[...] = lax.rsqrt(squares * (1.0 / WIDTH) + 1e-06) / math.sqrt(WIDTH)
+    products = None
     for k, (start, _, real) in enumerate(CHUNKS):
         inv_scale = lax.rsqrt(
             jnp.sum(sums[k] * sums[k], axis=1, keepdims=True) * (1.0 / WIDTH) + 1e-06
         ) / math.sqrt(WIDTH)
         unit = (sums[k] * inv_scale).astype(jnp.bfloat16)
-        centroids[pl.ds(start, real)] = unit[:real]
-        if k == len(CHUNKS) - 1:
-            stores.append(pltpu.make_async_copy(centroids, centroids_hbm, out_sem.at[0]))
-            stores[-1].start()
+        centroids_ref[pl.ds(start, real)] = unit[:real]
         similar = matmul(unit, rows, NT)
         part = jnp.sum(jnp.where(labels[k] == owner, similar, 0.0), axis=0, keepdims=True)
         products = part if products is None else products + part
@@ -171,22 +172,10 @@
     )
     square = (DEVICES, LANES)
     products_ref[...] = jnp.where(iota(square, 0) & (GROUP - 1) == iota(square, 1) >> 3, spread, 0.0)
-    stores.append(pltpu.make_async_copy(products_ref, products_hbm, out_sem.at[1]))
-    stores[-1].start()
-    load.wait()
-    total = None
-    for c in range(WIDTH // LANES):
-        piece = emb[:, c * LANES:(c + 1) * LANES].astype(jnp.float32)
-        total = piece * piece if total is None else total + piece * piece
-    squares = jnp.sum(total.T, axis=0, keepdims=True)
-    scale_ref[...] = lax.rsqrt(squares * (1.0 / WIDTH) + 1e-06) / math.sqrt(WIDTH)
-    for store in stores:
-        store.wait()
 
 
 def middle(arrived, embeddings):
     vmem = pl.BlockSpec(memory_space=pltpu.VMEM)
-    hbm = pl.BlockSpec(memory_space=pl.ANY)
     return pl.pallas_call(
         middle_kernel,
         out_shape=(
@@ -194,20 +183,17 @@
             jax.ShapeDtypeStruct((DEVICES, LANES), jnp.float32),
             jax.ShapeDtypeStruct((1, ROWS), jnp.float32),
         ),
-        in_specs=[vmem, hbm],
-        out_specs=(hbm, hbm, vmem),
-        scratch_shapes=[
-            pltpu.VMEM((ROWS, WIDTH), jnp.bfloat16),
-            pltpu.VMEM((CLUSTER_DEV, WIDTH), jnp.bfloat16),
-            pltpu.VMEM((DEVICES, LANES), jnp.float32),
-            pltpu.SemaphoreType.DMA,
-            pltpu.SemaphoreType.DMA((2,)),
-        ],
+        in_specs=[vmem, vmem],
+        out_specs=(vmem, vmem, vmem),
         compiler_params=pltpu.CompilerParams(vmem_limit_bytes=VMEM_LIMIT),
     )(arrived, embeddings)
 
 
-def final_kernel(returned_ref, slot_ref, scale_ref, scores_ref):
+def final_kernel(
+    returned_ref, slot_ref, scale_ref, centroids_ref, centroids_hbm, scores_hbm, scores, out_sem
+):
+    stores = [pltpu.make_async_copy(centroids_ref, centroids_hbm, out_sem.at[0])]
+    stores[-1].start()
     slot = slot_ref[...]
     hits = as_bf16(iota((DEVICES, ROWS), 0) == slot >> 3)
     back = jnp.sum(returned_ref[...].T.reshape(GROUP, CAP, DEVICES), axis=0)
@@ -216,18 +202,27 @@
         term = matmul(part, hits)
         total = term if total is None else total + term
     chosen = jnp.where(iota((CAP, ROWS), 0) == slot & (CAP - 1), total, 0.0)
-    scores_ref[...] = jnp.sum(chosen, axis=0, keepdims=True) * scale_ref[...]
-
-
-def final(returned, slot, scale):
+    scores[...] = jnp.sum(chosen, axis=0, keepdims=True) * scale_ref[...]
+    stores.append(pltpu.make_async_copy(scores, scores_hbm, out_sem.at[1]))
+    stores[-1].start()
+    for store in stores:
+        store.wait()
+
+
+def final(returned, slot, scale, centroids):
     vmem = pl.BlockSpec(memory_space=pltpu.VMEM)
+    hbm = pl.BlockSpec(memory_space=pl.ANY)
     return pl.pallas_call(
         final_kernel,
-        out_shape=jax.ShapeDtypeStruct((1, ROWS), jnp.float32),
-        in_specs=[vmem] * 3,
-        out_specs=vmem,
+        out_shape=(
+            jax.ShapeDtypeStruct((CLUSTER_DEV, WIDTH), jnp.bfloat16),
+            jax.ShapeDtypeStruct((1, ROWS), jnp.float32),
+        ),
+        in_specs=[vmem] * 4,
+        out_specs=(hbm, hbm),
+        scratch_shapes=[pltpu.VMEM((1, ROWS), jnp.float32), pltpu.SemaphoreType.DMA((2,))],
         compiler_params=pltpu.CompilerParams(vmem_limit_bytes=16 * 1024 * 1024),
-    )(returned, slot, scale)
+    )(returned, slot, scale, centroids)
 
 
 def body(embeddings, cluster_ids, keep_flags):
@@ -235,7 +230,7 @@
     arrived = lax.all_to_all(outgoing, AXES, split_axis=0, concat_axis=0, tiled=True)
     centroids, products, row_scale = middle(arrived, embeddings)
     returned = lax.all_to_all(products, AXES, split_axis=0, concat_axis=0, tiled=True)
-    scores = final(returned, slot, row_scale)
+    centroids, scores = final(returned, slot, row_scale, centroids)
     return (centroids, scores.reshape(ROWS))
 
 

time: 57.4 us -> 57 us (level)
  no operation moved by 1% of the time
where the time goes in v7:
time: 57 us; the launch traced here: 56.9 us
  blocking collectives  51.2 us (90%)
  Pallas kernels  5.06 us (9%)
  between operations  0.66 us (1%)
    all_to_all x1, blocking collectives, body(): lax.all_to_all(outgoing, AXES, split_axis=0, concat_axis=0, tiled=True)  37.7 us
    all_to_all x1, blocking collectives, body(): lax.all_to_all(products, AXES, split_axis=0, concat_axis=0, tiled=True)  13.5 us
    pallas_call x1, Pallas kernels, pack(): pl.pallas_call(pack_kernel, out_shape=(jax.ShapeDtypeStruct((DEVICES, DAT...  2.31 us
    pallas_call x1, Pallas kernels, middle(): pl.pallas_call(middle_kernel, out_shape=(jax.ShapeDtypeStruct((CLUSTER_DE...  1.89 us

profile of v7, /device:TPU:1, one launch (start us, length us, event | category | flops | bytes accessed | tf_op | source)
XLA Modules:
  0.0 56.9 jit_solution(704470684118814836)
XLA Ops:
  0.6 2.3 %shard_map.50 = (bf16[128,13,4,128]{3,2,1,0:T(4,128)(2,1)S(1)}, s32[1,512]{1,0:T(1,128)S(1)}) custom-call(s32[1,512]{1,0:T(1,128)} %bitcast.9, s32[1,512]{1,0:T(1,128)} %bitcast.10, bf16[512,768]{1,0:T(8,128)(2,1)} %emb.1), custom_call_target="tpu_custom_call" | custom-call | tf_op jit(solution)/shard_map/pallas_call | solution.py:115
  2.9 0.0 copy-start
  3.0 37.7 %all_to_all.16.arrived = bf16[128,13,4,128]{3,2,1,0:T(4,128)(2,1)S(1)} all-to-all(bf16[128,13,4,128]{3,2,1,0:T(4,128)(2,1)S(1)} %get-tuple-element.9), channel_id=1, replica_groups=mesh['doc'=16,'own'=8] {'doc','own'}, dimensions={0} | all-to-all | bytes 3407872 | tf_op jit(solution)/shard_map/all_to_all | solution.py:230
  40.6 0.0 copy-done
  40.6 1.9 %shard_map.51 = (bf16[392,768]{1,0:T(8,128)(2,1)S(1)}, f32[128,128]{1,0:T(8,128)S(1)}, f32[1,512]{1,0:T(1,128)S(1)}) custom-call(bf16[128,13,4,128]{3,2,1,0:T(4,128)(2,1)S(1)} %all_to_all.16.arrived, bf16[512,768]{1,0:T(8,128)(2,1)S(1)} %copy-done), custom_call_target="tpu_custom_call" | custom-call | tf_op jit(solution)/shard_map/pallas_call | solution.py:179
  42.5 13.5 %all_to_all.17 = f32[128,1,128]{2,1,0:T(1,128)S(1)} all-to-all(f32[128,1,128]{2,1,0:T(1,128)S(1)} %bitcast.8), channel_id=1, replica_groups=mesh['doc'=16,'own'=8] {'doc','own'}, dimensions={0} | all-to-all | bytes 131072 | tf_op jit(solution)/shard_map/all_to_all | solution.py:232
  56.0 0.9 %shard_map.52 = (bf16[392,768]{1,0:T(8,128)(2,1)}, f32[1,512]{1,0:T(1,128)}) custom-call(f32[128,128]{1,0:T(8,128)S(1)} %bitcast.7, s32[1,512]{1,0:T(1,128)S(1)} %get-tuple-element.11.slot_ref, f32[1,512]{1,0:T(1,128)S(1)} %get-tuple-element.12.scale_ref, bf16[392,768]{1,0:T(8,128)(2,1)S(1)} %get-tuple-element.13.centroids_ref), custom_call_target="tpu_custom_call" | custom-call | tf_op jit(solution)/shard_map/pallas_call | solution.py:215
Async XLA Ops:
  2.9 37.7 %copy-start = (bf16[512,768]{1,0:T(8,128)(2,1)S(1)}, bf16[512,768]{1,0:T(8,128)(2,1)}, u32[]{:S(2)}) copy-start(bf16[512,768]{1,0:T(8,128)(2,1)} %emb.1) | copy-start | bytes 2359300

commit v8 on v7

--- a/solution.py
+++ b/solution.py
@@ -197,10 +197,8 @@
     slot = slot_ref[...]
     hits = as_bf16(iota((DEVICES, ROWS), 0) == slot >> 3)
     back = jnp.sum(returned_ref[...].T.reshape(GROUP, CAP, DEVICES), axis=0)
-    total = None
-    for part in split3(back):
-        term = matmul(part, hits)
-        total = term if total is None else total + term
+    parts = matmul(jnp.concatenate(split3(back), axis=0), hits)
+    total = parts[:CAP] + parts[CAP:2 * CAP] + parts[2 * CAP:]
     chosen = jnp.where(iota((CAP, ROWS), 0) == slot & (CAP - 1), total, 0.0)
     scores[...] = jnp.sum(chosen, axis=0, keepdims=True) * scale_ref[...]
     stores.append(pltpu.make_async_copy(scores, scores_hbm, out_sem.at[1]))

time: 57 us -> 57 us (level)
  no operation moved by 1% of the time
where the time goes in v8:
time: 57 us; the launch traced here: 56.9 us
  blocking collectives  51.2 us (90%)
  Pallas kernels  5.04 us (9%)
  between operations  0.66 us (1%)
    all_to_all x1, blocking collectives, body(): lax.all_to_all(outgoing, AXES, split_axis=0, concat_axis=0, tiled=True)  37.7 us
    all_to_all x1, blocking collectives, body(): lax.all_to_all(products, AXES, split_axis=0, concat_axis=0, tiled=True)  13.5 us
    pallas_call x1, Pallas kernels, pack(): pl.pallas_call(pack_kernel, out_shape=(jax.ShapeDtypeStruct((DEVICES, DAT...  2.31 us
    pallas_call x1, Pallas kernels, middle(): pl.pallas_call(middle_kernel, out_shape=(jax.ShapeDtypeStruct((CLUSTER_DE...  1.89 us

profile of v8, /device:TPU:1, one launch (start us, length us, event | category | flops | bytes accessed | tf_op | source)
XLA Modules:
  0.0 56.9 jit_solution(13007658452813283062)
XLA Ops:
  0.6 2.3 %shard_map.50 = (bf16[128,13,4,128]{3,2,1,0:T(4,128)(2,1)S(1)}, s32[1,512]{1,0:T(1,128)S(1)}) custom-call(s32[1,512]{1,0:T(1,128)} %bitcast.9, s32[1,512]{1,0:T(1,128)} %bitcast.10, bf16[512,768]{1,0:T(8,128)(2,1)} %emb.1), custom_call_target="tpu_custom_call" | custom-call | tf_op jit(solution)/shard_map/pallas_call | solution.py:115
  2.9 0.0 copy-start
  3.0 37.7 %all_to_all.16.arrived = bf16[128,13,4,128]{3,2,1,0:T(4,128)(2,1)S(1)} all-to-all(bf16[128,13,4,128]{3,2,1,0:T(4,128)(2,1)S(1)} %get-tuple-element.9), channel_id=1, replica_groups=mesh['doc'=16,'own'=8] {'doc','own'}, dimensions={0} | all-to-all | bytes 3407872 | tf_op jit(solution)/shard_map/all_to_all | solution.py:228
  40.6 0.0 copy-done
  40.6 1.9 %shard_map.51 = (bf16[392,768]{1,0:T(8,128)(2,1)S(1)}, f32[128,128]{1,0:T(8,128)S(1)}, f32[1,512]{1,0:T(1,128)S(1)}) custom-call(bf16[128,13,4,128]{3,2,1,0:T(4,128)(2,1)S(1)} %all_to_all.16.arrived, bf16[512,768]{1,0:T(8,128)(2,1)S(1)} %copy-done), custom_call_target="tpu_custom_call" | custom-call | tf_op jit(solution)/shard_map/pallas_call | solution.py:179
  42.5 13.5 %all_to_all.17 = f32[128,1,128]{2,1,0:T(1,128)S(1)} all-to-all(f32[128,1,128]{2,1,0:T(1,128)S(1)} %bitcast.8), channel_id=1, replica_groups=mesh['doc'=16,'own'=8] {'doc','own'}, dimensions={0} | all-to-all | bytes 131072 | tf_op jit(solution)/shard_map/all_to_all | solution.py:230
  56.0 0.8 %shard_map.52 = (bf16[392,768]{1,0:T(8,128)(2,1)}, f32[1,512]{1,0:T(1,128)}) custom-call(f32[128,128]{1,0:T(8,128)S(1)} %bitcast.7, s32[1,512]{1,0:T(1,128)S(1)} %get-tuple-element.11.slot_ref, f32[1,512]{1,0:T(1,128)S(1)} %get-tuple-element.12.scale_ref, bf16[392,768]{1,0:T(8,128)(2,1)S(1)} %get-tuple-element.13.centroids_ref), custom_call_target="tpu_custom_call" | custom-call | tf_op jit(solution)/shard_map/pallas_call | solution.py:213
Async XLA Ops:
  2.9 37.7 %copy-start = (bf16[512,768]{1,0:T(8,128)(2,1)S(1)}, bf16[512,768]{1,0:T(8,128)(2,1)}, u32[]{:S(2)}) copy-start(bf16[512,768]{1,0:T(8,128)(2,1)} %emb.1) | copy-start | bytes 2359300

commit v9 on v8

--- a/solution.py
+++ b/solution.py
@@ -9,7 +9,7 @@
 
 AXES = ("doc", "own")
 CLUSTER_DEV = 392
-CHUNKS = ((0, 208, 208), (208, 192, 184))
+CHUNKS = ((0, 192, 192), (192, 200, 200))
 DEVICES = 128
 CAP = 8
 SLOTS = DEVICES * CAP

time: 57 us -> 57 us (level)
  no operation moved by 1% of the time
where the time goes in v9:
time: 57 us; the launch traced here: 56.9 us
  blocking collectives  51.2 us (90%)
  Pallas kernels  5.05 us (9%)
  between operations  0.66 us (1%)
    all_to_all x1, blocking collectives, body(): lax.all_to_all(outgoing, AXES, split_axis=0, concat_axis=0, tiled=True)  37.7 us
    all_to_all x1, blocking collectives, body(): lax.all_to_all(products, AXES, split_axis=0, concat_axis=0, tiled=True)  13.5 us
    pallas_call x1, Pallas kernels, pack(): pl.pallas_call(pack_kernel, out_shape=(jax.ShapeDtypeStruct((DEVICES, DAT...  2.31 us
    pallas_call x1, Pallas kernels, middle(): pl.pallas_call(middle_kernel, out_shape=(jax.ShapeDtypeStruct((CLUSTER_DE...  1.9 us

profile of v9, /device:TPU:1, one launch (start us, length us, event | category | flops | bytes accessed | tf_op | source)
XLA Modules:
  0.0 56.9 jit_solution(15582921441970346152)
XLA Ops:
  0.6 2.3 %shard_map.50 = (bf16[128,13,4,128]{3,2,1,0:T(4,128)(2,1)S(1)}, s32[1,512]{1,0:T(1,128)S(1)}) custom-call(s32[1,512]{1,0:T(1,128)} %bitcast.9, s32[1,512]{1,0:T(1,128)} %bitcast.10, bf16[512,768]{1,0:T(8,128)(2,1)} %emb.1), custom_call_target="tpu_custom_call" | custom-call | tf_op jit(solution)/shard_map/pallas_call | solution.py:115
  2.9 0.0 copy-start
  3.0 37.7 %all_to_all.16.arrived = bf16[128,13,4,128]{3,2,1,0:T(4,128)(2,1)S(1)} all-to-all(bf16[128,13,4,128]{3,2,1,0:T(4,128)(2,1)S(1)} %get-tuple-element.9), channel_id=1, replica_groups=mesh['doc'=16,'own'=8] {'doc','own'}, dimensions={0} | all-to-all | bytes 3407872 | tf_op jit(solution)/shard_map/all_to_all | solution.py:228
  40.6 0.0 copy-done
  40.6 1.9 %shard_map.51 = (bf16[392,768]{1,0:T(8,128)(2,1)S(1)}, f32[128,128]{1,0:T(8,128)S(1)}, f32[1,512]{1,0:T(1,128)S(1)}) custom-call(bf16[128,13,4,128]{3,2,1,0:T(4,128)(2,1)S(1)} %all_to_all.16.arrived, bf16[512,768]{1,0:T(8,128)(2,1)S(1)} %copy-done), custom_call_target="tpu_custom_call" | custom-call | tf_op jit(solution)/shard_map/pallas_call | solution.py:179
  42.5 13.5 %all_to_all.17 = f32[128,1,128]{2,1,0:T(1,128)S(1)} all-to-all(f32[128,1,128]{2,1,0:T(1,128)S(1)} %bitcast.8), channel_id=1, replica_groups=mesh['doc'=16,'own'=8] {'doc','own'}, dimensions={0} | all-to-all | bytes 131072 | tf_op jit(solution)/shard_map/all_to_all | solution.py:230
  56.0 0.8 %shard_map.52 = (bf16[392,768]{1,0:T(8,128)(2,1)}, f32[1,512]{1,0:T(1,128)}) custom-call(f32[128,128]{1,0:T(8,128)S(1)} %bitcast.7, s32[1,512]{1,0:T(1,128)S(1)} %get-tuple-element.11.slot_ref, f32[1,512]{1,0:T(1,128)S(1)} %get-tuple-element.12.scale_ref, bf16[392,768]{1,0:T(8,128)(2,1)S(1)} %get-tuple-element.13.centroids_ref), custom_call_target="tpu_custom_call" | custom-call | tf_op jit(solution)/shard_map/pallas_call | solution.py:213
Async XLA Ops:
  2.9 37.7 %copy-start = (bf16[512,768]{1,0:T(8,128)(2,1)S(1)}, bf16[512,768]{1,0:T(8,128)(2,1)}, u32[]{:S(2)}) copy-start(bf16[512,768]{1,0:T(8,128)(2,1)} %emb.1) | copy-start | bytes 2359300

commit v10 on v9

--- a/solution.py
+++ b/solution.py
@@ -9,7 +9,7 @@
 
 AXES = ("doc", "own")
 CLUSTER_DEV = 392
-CHUNKS = ((0, 192, 192), (192, 200, 200))
+CHUNKS = ((0, 208, 208), (208, 184, 184))
 DEVICES = 128
 CAP = 8
 SLOTS = DEVICES * CAP

time: 57 us -> 57 us (level)
  no operation moved by 1% of the time
where the time goes in v10:
time: 57 us; the launch traced here: 56.9 us
  blocking collectives  51.2 us (90%)
  Pallas kernels  5.04 us (9%)
  between operations  0.66 us (1%)
    all_to_all x1, blocking collectives, body(): lax.all_to_all(outgoing, AXES, split_axis=0, concat_axis=0, tiled=True)  37.7 us
    all_to_all x1, blocking collectives, body(): lax.all_to_all(products, AXES, split_axis=0, concat_axis=0, tiled=True)  13.5 us
    pallas_call x1, Pallas kernels, pack(): pl.pallas_call(pack_kernel, out_shape=(jax.ShapeDtypeStruct((DEVICES, DAT...  2.31 us
    pallas_call x1, Pallas kernels, middle(): pl.pallas_call(middle_kernel, out_shape=(jax.ShapeDtypeStruct((CLUSTER_DE...  1.89 us

profile of v10, /device:TPU:1, one launch (start us, length us, event | category | flops | bytes accessed | tf_op | source)
XLA Modules:
  0.0 56.9 jit_solution(14064798948348265628)
XLA Ops:
  0.6 2.3 %shard_map.50 = (bf16[128,13,4,128]{3,2,1,0:T(4,128)(2,1)S(1)}, s32[1,512]{1,0:T(1,128)S(1)}) custom-call(s32[1,512]{1,0:T(1,128)} %bitcast.9, s32[1,512]{1,0:T(1,128)} %bitcast.10, bf16[512,768]{1,0:T(8,128)(2,1)} %emb.1), custom_call_target="tpu_custom_call" | custom-call | tf_op jit(solution)/shard_map/pallas_call | solution.py:115
  2.9 0.0 copy-start
  3.0 37.7 %all_to_all.16.arrived = bf16[128,13,4,128]{3,2,1,0:T(4,128)(2,1)S(1)} all-to-all(bf16[128,13,4,128]{3,2,1,0:T(4,128)(2,1)S(1)} %get-tuple-element.9), channel_id=1, replica_groups=mesh['doc'=16,'own'=8] {'doc','own'}, dimensions={0} | all-to-all | bytes 3407872 | tf_op jit(solution)/shard_map/all_to_all | solution.py:228
  40.6 0.0 copy-done
  40.6 1.9 %shard_map.51 = (bf16[392,768]{1,0:T(8,128)(2,1)S(1)}, f32[128,128]{1,0:T(8,128)S(1)}, f32[1,512]{1,0:T(1,128)S(1)}) custom-call(bf16[128,13,4,128]{3,2,1,0:T(4,128)(2,1)S(1)} %all_to_all.16.arrived, bf16[512,768]{1,0:T(8,128)(2,1)S(1)} %copy-done), custom_call_target="tpu_custom_call" | custom-call | tf_op jit(solution)/shard_map/pallas_call | solution.py:179
  42.5 13.5 %all_to_all.17 = f32[128,1,128]{2,1,0:T(1,128)S(1)} all-to-all(f32[128,1,128]{2,1,0:T(1,128)S(1)} %bitcast.8), channel_id=1, replica_groups=mesh['doc'=16,'own'=8] {'doc','own'}, dimensions={0} | all-to-all | bytes 131072 | tf_op jit(solution)/shard_map/all_to_all | solution.py:230
  56.0 0.8 %shard_map.52 = (bf16[392,768]{1,0:T(8,128)(2,1)}, f32[1,512]{1,0:T(1,128)}) custom-call(f32[128,128]{1,0:T(8,128)S(1)} %bitcast.7, s32[1,512]{1,0:T(1,128)S(1)} %get-tuple-element.11.slot_ref, f32[1,512]{1,0:T(1,128)S(1)} %get-tuple-element.12.scale_ref, bf16[392,768]{1,0:T(8,128)(2,1)S(1)} %get-tuple-element.13.centroids_ref), custom_call_target="tpu_custom_call" | custom-call | tf_op jit(solution)/shard_map/pallas_call | solution.py:213
Async XLA Ops:
  2.9 37.7 %copy-start = (bf16[512,768]{1,0:T(8,128)(2,1)S(1)}, bf16[512,768]{1,0:T(8,128)(2,1)}, u32[]{:S(2)}) copy-start(bf16[512,768]{1,0:T(8,128)(2,1)} %emb.1) | copy-start | bytes 2359300
